TPU v7x, 32 devices: a whole 2x2x4 slice. The times are simulated.
32 devices in a mesh: grp: 2 (over y), blk: 8 (over z, x), pair: 2 (over core).
Axes of the slice: x: 2, y: 2, z: 4, core: 2. Of those that a mesh axis runs over, the one named last changes fastest.
Arguments:
- wavefunc: bfloat16 [96, 16, 2, 768], P(('grp', 'blk')), parts along dimension 0, may hold values from -6 to 6
- haydock: float32 [96, 128], P(('grp', 'blk')), parts along dimension 0, may hold values from -6 to 6
- screened: bfloat16 [16, 768, 768], P(('grp', 'blk')), parts along dimension 0, may hold values from -0.21875 to 0.21875
- coulomb: float32 [1536], P('grp'), parts along dimension 0, may hold values from 0.05 to 1
- umklapp_map: int32 [3, 768], replicated, may hold values from 0 to 767, each once within a row
Outputs:
- kernel_out: float32 [96, 128], P(('grp', 'blk')), parts along dimension 0
There are 2 independent parts, one for each index of `grp`. A program takes and returns all parts, laid end to end along the dimension named above; an argument that names none is the same for every part. Nothing has to cross between parts.
Inputs may be any that keep to these rules, and one draw needn't show every extreme that they name: Each row of umklapp_map is a permutation of 0 .. 767.
All inputs are finite; a program needn't handle non-finite values.
Results may differ from a plain program's by a relative error of at most 0.015.
Values may be sent and summed in bfloat16 or wider, within the bound.
A program may use at most 64 MiB of HBM per device.

v0:
```python
import functools
import math

import jax
import jax.numpy as jnp
from jax import lax
from jax.experimental import pallas as pl
from jax.experimental.pallas import tpu as pltpu
from jax.sharding import PartitionSpec as P

NV = 8
NC = 8
STOPS = 2
MESH = pl.DeviceIdType.MESH
NT = (((1,), (1,)), ((), ()))


def dot_nt(a, b):
    return lax.dot_general(a, b, NT, preferred_element_type=jnp.float32)


def dot_nn(a, b):
    return jnp.dot(a, b, preferred_element_type=jnp.float32)


def make_pieces(wave, hay):
    count, bands, _, planes = wave.shape
    rows = wave.reshape(count, 2, NV, 2, planes).transpose(1, 3, 0, 2, 4)
    rows = rows.reshape(2, 2 * count * NV, planes)
    psi = hay.reshape(count, 2, NV, NC).transpose(1, 0, 3, 2)
    eye = jnp.eye(count, dtype=jnp.float32)
    wide = (psi[:, :, :, None, :] * eye[None, :, None, :, None]).reshape(2, count * NC, count * NV)
    top = jnp.concatenate([wide[0], -wide[1]], axis=1)
    low = jnp.concatenate([wide[1], wide[0]], axis=1)
    mix = jnp.concatenate([top, low], axis=0).astype(jnp.bfloat16)
    return rows, mix


def unpack_result(total, count):
    half = count * NC
    out_re = total[:NV, :half] - total[NV:, half : 2 * half]
    out_im = total[NV:, :half] + total[:NV, half : 2 * half]
    out = jnp.stack([out_re, out_im]).reshape(2, NV, count, NC)
    return out.transpose(2, 0, 1, 3).reshape(count, 2 * NV * NC)


def fold_rows(f_rows, cond, count):
    t = dot_nt(f_rows, cond)
    rows, lanes = t.shape
    keep = (lax.broadcasted_iota(jnp.int32, t.shape, 0) // NV) % count == (
        lax.broadcasted_iota(jnp.int32, t.shape, 1) // NC
    ) % count
    t = jnp.where(keep, t, 0.0).reshape(2, count, NV, lanes)
    return jnp.sum(t, axis=1).reshape(2 * NV, lanes)


def kernel(
    count, scale_d, scale_x,
    piece_ref, weight_ref, map_ref, coul_ref, out_ref,
    ubuf, sel, fbuf, stage, res, xbuf,
    recv_near, recv_peer, send_piece, send_res, recv_res, send_x, recv_x,
):
    grp = lax.axis_index("grp")
    me = lax.axis_index("blk")
    p = lax.axis_index("pair")
    blocks = lax.axis_size("blk")
    z = me // 2
    x = me % 2
    worker = me < STOPS + 1
    planes = weight_ref.shape[0]
    half = planes // 2
    edge = count * NV

    barrier = pltpu.get_barrier_semaphore()
    for d in range(1, 2 * blocks):
        other = (me * 2 + p + d) % (2 * blocks)
        pl.semaphore_signal(barrier, inc=1, device_id=(grp, other // 2, other % 2), device_id_type=MESH)
    ubuf[me] = piece_ref[...]
    pl.semaphore_wait(barrier, 2 * blocks - 1)

    def routes(b):
        zb = b // 2
        xb = b % 2
        return (
            (worker & (b != me), me, 1 - p, recv_peer),
            ((b == me) & (me != 2), 2, p, recv_near),
            ((b == me) & (me != 1), 1, p, recv_near),
            ((b == me) & (me != 0), 0, p, recv_near),
        )

    widths = (ubuf.shape[3], planes)

    def piece(b, h):
        return ubuf.at[b, h, :, pl.ds(0, widths[h])]

    def copy_of(b, h, kind, target, core, sems):
        return pltpu.make_async_remote_copy(
            src_ref=piece(b, h),
            dst_ref=piece(b, h),
            send_sem=send_piece.at[kind, b],
            recv_sem=sems.at[b],
            device_id=(grp, target, core),
            device_id_type=MESH,
        )

    def forward(b):
        for kind, (go, target, core, sems) in enumerate(routes(b)):
            for h in range(2):
                @pl.when(go & (p == h))
                def _():
                    copy_of(b, h, kind, target, core, sems).start()

    def drain(b):
        for kind, (go, target, core, sems) in enumerate(routes(b)):
            for h in range(2):
                @pl.when(go & (p == h))
                def _():
                    copy_of(b, h, kind, target, core, sems).wait_send()

    def arrive(b):
        for h in range(2):
            @pl.when(p == h)
            def _():
                pltpu.make_async_copy(piece(b, h), piece(b, h), recv_near.at[b]).wait()
        forward(b)

    def arrive_peer(b):
        for h in range(2):
            @pl.when(p == 1 - h)
            def _():
                pltpu.make_async_copy(piece(b, h), piece(b, h), recv_peer.at[b]).wait()

    forward(me)

    cond_own = piece_ref[1, :, :planes].astype(jnp.float32)
    amp = dot_nn(piece_ref[0, :, planes : planes + 2 * edge], piece_ref[0, :, :planes])
    c_re, c_im = cond_own[:edge], cond_own[edge:]
    a_re, a_im = amp[:edge], amp[edge:]
    xbuf[me, 0:1, :] = jnp.sum(c_re * a_re + c_im * a_im, axis=0, keepdims=True)
    xbuf[me, 1:2, :] = jnp.sum(c_re * a_im - c_im * a_re, axis=0, keepdims=True)

    def x_copy(d):
        return pltpu.make_async_remote_copy(
            src_ref=xbuf.at[me],
            dst_ref=xbuf.at[me],
            send_sem=send_x.at[d],
            recv_sem=recv_x.at[me],
            device_id=(grp, (me + d) % blocks, p),
            device_id_type=MESH,
        )

    for d in range(1, blocks):
        x_copy(d).start()

    def res_copy(b, core):
        return pltpu.make_async_remote_copy(
            src_ref=stage.at[b],
            dst_ref=res.at[me * 2 + p],
            send_sem=send_res.at[b, core],
            recv_sem=recv_res.at[me * 2 + p],
            device_id=(grp, b, core),
            device_id_type=MESH,
        )

    @pl.when(worker)
    def _():
        s = me
        base = pl.multiple_of(p * half, 128)
        sel[...] = jnp.where(
            map_ref[...] == lax.broadcasted_iota(jnp.int32, (planes, planes), 1), 1.0, 0.0
        ).astype(jnp.bfloat16)

        def step(t, carry):
            i = t
            b = (i + s) % blocks
            first = jnp.where((s >= 1) & (t == 0), 0, jnp.where((s == 2) & (t == 1), 1, b))
            take = ((s == 0) & (t >= 1)) | ((s == 1) & (t <= 6)) | ((s == 2) & (t <= 5))

            @pl.when(t == 0)
            def _():
                for near in range(blocks // 2):
                    @pl.when(near != me)
                    def _():
                        arrive(near)

            @pl.when(take & (first == blocks // 2))
            def _():
                for far in range(blocks // 2, blocks):
                    arrive(far)

            @pl.when(take)
            def _():
                arrive_peer(first)

            @pl.when((s == 2) & (t == 1))
            def _():
                arrive_peer(3)

            val_j = ubuf[i, 0, :, :planes]
            mix_j = ubuf[i, 0, :, planes : planes + 2 * edge]
            amp_j = dot_nn(mix_j, val_j).astype(jnp.bfloat16)
            perm = dot_nt(amp_j, sel[...])
            perm_re = perm.astype(jnp.bfloat16)
            perm_im = jnp.concatenate([perm[edge:], -perm[:edge]], axis=0).astype(jnp.bfloat16)
            cond_t = dot_nt(sel[pl.ds(base, half), :], ubuf[i, 1, :, :planes]).astype(jnp.bfloat16)
            val_b = ubuf[b, 0, :, :planes]
            tile = 128
            for r in range(half // tile):
                rows = pl.ds(pl.multiple_of(base + r * tile, 128), tile)
                w = weight_ref[rows, :].astype(jnp.float32)
                left = cond_t[r * tile : (r + 1) * tile]
                h_re = (dot_nn(left, perm_re) * w).astype(jnp.bfloat16)
                h_im = (dot_nn(left, perm_im) * w).astype(jnp.bfloat16)
                g_re = dot_nt(val_b, h_re)
                g_im = dot_nt(val_b, h_im)
                f_re = g_re[:edge] + g_im[edge:]
                f_im = g_im[:edge] - g_re[edge:]
                fbuf[:, r * tile : (r + 1) * tile] = (
                    jnp.concatenate([f_re, f_im], axis=0) * scale_d
                ).astype(jnp.bfloat16)
            cond_b = ubuf[b, 1, :, pl.ds(base, half)]
            part = fold_rows(fbuf[...], cond_b, count)
            stage[b, :, : 2 * edge] = part
            for core in range(2):
                mine = (b == me) & (p == core)

                @pl.when(mine)
                def _():
                    res[me * 2 + p, :, : 2 * edge] = part

                @pl.when(jnp.logical_not(mine))
                def _():
                    res_copy(b, core).start()

            return carry

        lax.fori_loop(0, blocks, step, 0)

    for d in range(1, blocks):
        src = (me + d) % blocks
        pltpu.make_async_copy(xbuf.at[src], xbuf.at[src], recv_x.at[src]).wait()
    y = jnp.sum(xbuf[...], axis=0) * coul_ref[...] * scale_x
    y_re, y_im = y[0:1], y[1:2]
    v_re = piece_ref[0, :edge, :planes].astype(jnp.float32)
    v_im = piece_ref[0, edge:, :planes].astype(jnp.float32)
    f_rows = jnp.concatenate([y_re * v_re + y_im * v_im, y_im * v_re - y_re * v_im], axis=0)
    total = fold_rows(f_rows.astype(jnp.bfloat16), piece_ref[1, :, :planes], count)

    for slot in range(2 * (STOPS + 1)):
        @pl.when(slot != me * 2 + p)
        def _():
            pltpu.make_async_copy(res.at[slot], res.at[slot], recv_res.at[slot]).wait()
    for slot in range(2 * (STOPS + 1)):
        total = total + res[slot, :, : 2 * edge]
    out_ref[...] = total

    for b in range(blocks):
        @pl.when(worker | ((b % 2 == x) & (b // 2 >= z)))
        def _():
            drain(b)
    for d in range(1, blocks):
        x_copy(d).wait_send()

    @pl.when(worker)
    def _():
        for b in range(blocks):
            for core in range(2):
                @pl.when(jnp.logical_not((b == me) & (p == core)))
                def _():
                    res_copy(b, core).wait_send()


def scales(planes, count, total_k):
    return (
        -1.0 / (8.0 * math.sqrt(planes * count * (STOPS + 1))),
        1.0 / (8.0 * math.sqrt(planes * total_k)),
    )


def per_device(wavefunc, haydock, screened, coulomb, umklapp_map):
    count, _, _, planes = wavefunc.shape
    blocks = lax.axis_size("blk")
    edge = count * NV
    rows, mix = make_pieces(wavefunc, haydock)
    mix = jnp.pad(mix, ((0, 0), (0, -2 * edge % 128)))
    pieces = jnp.concatenate([rows, jnp.stack([mix, jnp.zeros_like(mix)])], axis=2)
    stop = jnp.minimum(lax.axis_index("blk"), STOPS)
    index = lax.dynamic_index_in_dim(umklapp_map, stop, 0, keepdims=False).reshape(planes, 1)
    scale_d, scale_x = scales(planes, count, count * blocks)
    lanes = pieces.shape[2]
    vmem = pl.BlockSpec(memory_space=pltpu.VMEM)
    total = pl.pallas_call(
        functools.partial(kernel, count, scale_d, scale_x),
        out_shape=jax.ShapeDtypeStruct((2 * NV, 2 * edge), jnp.float32),
        in_specs=[vmem] * 4,
        out_specs=vmem,
        scratch_shapes=[
            pltpu.VMEM((blocks, 2, 2 * edge, lanes), jnp.bfloat16),
            pltpu.VMEM((planes, planes), jnp.bfloat16),
            pltpu.VMEM((2 * edge, planes // 2), jnp.bfloat16),
            pltpu.VMEM((blocks, 2 * NV, 128), jnp.float32),
            pltpu.VMEM((2 * (STOPS + 1), 2 * NV, 128), jnp.float32),
            pltpu.VMEM((blocks, 2, planes), jnp.float32),
            pltpu.SemaphoreType.DMA((blocks,)),
            pltpu.SemaphoreType.DMA((blocks,)),
            pltpu.SemaphoreType.DMA((4, blocks)),
            pltpu.SemaphoreType.DMA((blocks, 2)),
            pltpu.SemaphoreType.DMA((2 * (STOPS + 1),)),
            pltpu.SemaphoreType.DMA((blocks,)),
            pltpu.SemaphoreType.DMA((blocks,)),
        ],
        compiler_params=pltpu.CompilerParams(
            collective_id=0, has_side_effects=True, vmem_limit_bytes=40 * 1024 * 1024
        ),
    )(pieces, screened[0], index, coulomb.reshape(1, planes))
    return unpack_result(total, count)


def per_device_general(wavefunc, haydock, screened, coulomb, umklapp_map):
    count, _, _, planes = wavefunc.shape
    blocks = lax.axis_size("blk")
    edge = count * NV
    rows, mix = make_pieces(wavefunc, haydock)
    val, cond = rows[0], rows[1]
    amp = dot_nn(mix, val)
    wide = cond.astype(jnp.float32)
    c_re, c_im, a_re, a_im = wide[:edge], wide[edge:], amp[:edge], amp[edge:]
    x_re = jnp.sum(c_re * a_re + c_im * a_im, axis=0)
    x_im = jnp.sum(c_re * a_im - c_im * a_re, axis=0)
    xs = lax.psum(jnp.stack([x_re, x_im]), "blk")
    scale_d, scale_x = scales(planes, count, count * blocks)
    y = xs * coulomb * scale_x
    v_re, v_im = val[:edge].astype(jnp.float32), val[edge:].astype(jnp.float32)
    f = jnp.concatenate([y[0] * v_re + y[1] * v_im, y[1] * v_re - y[0] * v_im], axis=0)
    current = jnp.concatenate([amp.astype(jnp.bfloat16), cond], axis=0)
    for stop in range(STOPS + 1):
        if stop > 0:
            current = lax.ppermute(current, "blk", [(i, (i + 1) % blocks) for i in range(blocks)])
        held = lax.axis_index("blk") == stop
        weight = lax.psum(jnp.where(held, screened[0], jnp.zeros_like(screened[0])), "blk")
        pick = (umklapp_map[stop][:, None] == jnp.arange(planes)[None, :]).astype(jnp.bfloat16)
        perm = dot_nt(current, pick).astype(jnp.bfloat16)
        amp_p, cond_t = perm[: 2 * edge], perm[2 * edge :].T
        turned = jnp.concatenate([amp_p[edge:], -amp_p[:edge]], axis=0)
        h_re = (dot_nn(cond_t, amp_p) * weight.astype(jnp.float32)).astype(jnp.bfloat16)
        h_im = (dot_nn(cond_t, turned) * weight.astype(jnp.float32)).astype(jnp.bfloat16)
        g_re, g_im = dot_nt(val, h_re), dot_nt(val, h_im)
        f = f + scale_d * jnp.concatenate([g_re[:edge] + g_im[edge:], g_im[:edge] - g_re[edge:]], axis=0)
    return unpack_result(fold_rows(f.astype(jnp.bfloat16), cond, count), count)


def solution(mesh):
    placed = (
        P(("grp", "blk"), None, None, None),
        P(("grp", "blk"), None),
        P(("grp", "blk"), None, None),
        P("grp"),
        P(),
    )
    body = per_device if mesh.shape["blk"] == 8 and mesh.shape["pair"] == 2 else per_device_general
    return jax.shard_map(
        body, mesh=mesh, in_specs=placed, out_specs=P(("grp", "blk"), None), check_vma=False
    )
```

profile of v0, /device:TPU:0, one launch (start us, length us, event | category | flops | bytes accessed | tf_op | source)
XLA Modules:
  0.0 42.5 jit_solution(10064208318897582183)
XLA Ops:
  0.0 0.0 copy-start
  0.0 0.0 copy-start.2
  0.0 0.8 %reshape.40 = f32[6,2,8,8]{3,2,1,0:T(8,128)S(1)} reshape(f32[6,128]{1,0:T(8,128)} %param.6) | data formatting | bytes 6144 | tf_op jit(solution)/shard_map/reshape | solution.py:30
  0.8 0.1 copy.13
  0.9 0.1 broadcast_multiply_fusion
  1.1 0.0 copy-start.3
  1.1 0.0 copy-start.1
  1.1 0.1 reshape.44
  1.2 0.1 reshape.46
  1.3 0.1 reshape.47
  1.5 0.1 fusion.8
  1.6 0.0 copy-done.2
  1.6 0.0 copy-done
  1.7 0.2 copy.14.map_ref
  1.9 0.0 copy-done.3
  1.9 0.5 %copy-done.1 = bf16[1,768,768]{2,1,0:T(8,128)(2,1)S(1)} copy-done((bf16[1,768,768]{2,1,0:T(8,128)(2,1)S(1)}, bf16[1,768,768]{2,1,0:T(8,128)(2,1)}, u32[]{:S(2)}) %copy-start.1) | copy-done | bytes 1179672
  2.3 39.2 %shard_map.55 = f32[16,96]{1,0:T(8,128)S(1)} custom-call(bf16[2,96,896]{2,1,0:T(8,128)(2,1)S(1)} %fusion.1.piece_ref, bf16[768,768]{1,0:T(8,128)(2,1)S(1)} %bitcast.14, s32[768,1]{1,0:T(8,128)S(1)} %copy.14.map_ref, f32[1,768]{1,0:T(1,128)S(1)} %reshape.42.coul_ref), custom_call_target="tpu_custom_call" | custom-call | tf_op jit(solution)/shard_map/pallas_call | solution.py:292
  41.5 0.1 slice_subtract_fusion
  41.6 0.1 stack.18
  41.7 0.1 stack.17
  41.8 0.7 %reshape.43 = f32[6,128]{1,0:T(8,128)} reshape(f32[6,2,8,8]{3,2,1,0:T(8,128)S(1)} %copy.15) | data formatting | bytes 6144 | tf_op jit(solution)/shard_map/reshape | solution.py:44
  (9 shorter events, 0.2 us)
Async XLA Ops:
  0.0 1.6 %copy-start = (s32[3,768]{1,0:T(4,128)S(1)}, s32[3,768]{1,0:T(4,128)}, u32[]{:S(2)}) copy-start(s32[3,768]{1,0:T(4,128)} %param.9) | copy-start | bytes 27652
  0.0 1.6 %copy-start.2 = (bf16[6,16,2,768]{3,2,1,0:T(2,128)(2,1)S(1)}, bf16[6,16,2,768]{3,2,1,0:T(2,128)(2,1)}, u32[]{:S(2)}) copy-start(bf16[6,16,2,768]{3,2,1,0:T(2,128)(2,1)} %param.5) | copy-start | bytes 884740
  1.1 0.8 %copy-start.3 = (f32[768]{0:T(1024)S(1)}, f32[768]{0:T(1024)}, u32[]{:S(2)}) copy-start(f32[768]{0:T(1024)} %param.8) | copy-start | bytes 9220
  1.1 1.3 %copy-start.1 = (bf16[1,768,768]{2,1,0:T(8,128)(2,1)S(1)}, bf16[1,768,768]{2,1,0:T(8,128)(2,1)}, u32[]{:S(2)}) copy-start(bf16[1,768,768]{2,1,0:T(8,128)(2,1)} %param.7) | copy-start | bytes 3538948
where the time goes:
time: 42.6 us; the launch traced here: 42.5 us
  Pallas kernels  39.2 us (92%)
  local copies, waits for them, and re-layouts  2.81 us (7%)
    pallas_call x1, Pallas kernels, per_device(): pl.pallas_call(functools.partial(kernel, count, scale_d, scale_x), out_sh...  39.2 us

commit v1 on v0

v1 whole, which is shorter than its diff:
```python
import functools
import math

import jax
import jax.numpy as jnp
from jax import lax
from jax.experimental import pallas as pl
from jax.experimental.pallas import tpu as pltpu
from jax.sharding import PartitionSpec as P

NV = 8
NC = 8
STOPS = 2
MESH = pl.DeviceIdType.MESH
NT = (((1,), (1,)), ((), ()))

OWN = {
    0: ((1, 0), (1, 1), (2, 0)),
    1: ((0, 1), (2, 1)),
    2: ((0, 0),),
    3: ((1, 0), (2, 1)),
    4: ((0, 0), (2, 0)),
    5: ((1, 1), (2, 1)),
    6: ((2, 0), (0, 0)),
    7: ((1, 1), (2, 1)),
}
UNITS = {
    (0, 0): ((0, ()), (2, ((2, (1, 0)),)), (4, ((4, (1, 1)),)), (6, ((6, (1, 1)),))),
    (0, 1): ((1, ((1, None),)), (3, ((3, None),)), (5, ((5, None),)), (7, ((7, None),))),
    (1, 0): ((0, ((0, None),)), (1, ((3, (0, 1)), (2, None))), (2, ()), (3, ((4, None),))),
    (1, 1): ((7, ((0, None), (5, (0, 1)), (7, (0, 1)))), (4, ((4, (1, 0)),)), (5, ((6, None),)), (6, ())),
    (2, 0): ((0, ((0, None),)), (2, ((4, None),)), (6, ((6, None),)), (4, ())),
    (2, 1): ((1, ((1, None), (3, None))), (3, ((5, None),)), (7, ((7, None),)), (5, ())),
}
HUB = (0, 1)
ACTIONS = 3


def edges():
    to = {}
    for blk, targets in OWN.items():
        for target in targets:
            for core in range(2):
                to.setdefault(target, set()).add((blk, core))
    for worker, units in UNITS.items():
        for _, actions in units:
            for _, target in actions:
                if target is not None:
                    to.setdefault(target, set()).add(worker)
    for blk in range(8):
        for core in range(2):
            if (blk, core) != HUB:
                to.setdefault(HUB, set()).add((blk, core))
    for blk in range(STOPS + 1):
        to.setdefault((blk, 1), set()).add((blk, 0))
    return to


def dot_nt(a, b):
    return lax.dot_general(a, b, NT, preferred_element_type=jnp.float32)


def dot_nn(a, b):
    return jnp.dot(a, b, preferred_element_type=jnp.float32)


def lut(index, values):
    out = jnp.int32(0)
    for n, value in enumerate(values):
        if value:
            out = jnp.where(index == n, jnp.int32(value), out)
    return out


def iota(shape, dim):
    return lax.broadcasted_iota(jnp.int32, shape, dim)


def spread_matrix(edge):
    half = edge
    row, col = iota((128, 256), 0), iota((128, 256), 1)
    lane = col % 128
    y = (lane >= half).astype(jnp.int32)
    part = jnp.where(col >= 128, 1 - y, y)
    return ((row // 64 == part) & ((row % 64) // NC == lane % NV)).astype(jnp.bfloat16)


def make_mix(hay, spread, count):
    edge = count * NV
    tall = jnp.concatenate(
        [jnp.broadcast_to(hay[k : k + 1, :], (NC, 128)) for _ in range(2) for k in range(count)], axis=0
    )
    shape = (2 * edge, 128)
    row, col = iota(shape, 0), iota(shape, 1)
    tall = jnp.where(row % NC == col % NC, tall, 0.0).astype(jnp.bfloat16)
    q = dot_nn(tall, spread)
    top = row < edge
    k_row = jnp.where(top, row, row - edge) // NC
    k_col = jnp.where(col < edge, col, col - edge) // NV
    mix = jnp.where(top, jnp.where(col < edge, q[:, :128], -q[:, :128]), q[:, 128:])
    keep = (k_row == k_col) & (col < 2 * edge)
    return jnp.where(keep, mix, 0.0).astype(jnp.bfloat16)[:, : 2 * edge]


def fold_block(t, count):
    edge = count * NV
    row, col = iota(t.shape, 0), iota(t.shape, 1)
    k_row = jnp.where(row < edge, row, row - edge) // NC
    k_col = jnp.where(col < edge, col, col - edge) // NV
    t = jnp.where(k_row == k_col, t, 0.0)
    halves = []
    for x in range(2):
        acc = t[x * edge : x * edge + NC]
        for k in range(1, count):
            acc = acc + t[x * edge + k * NC : x * edge + (k + 1) * NC]
        halves.append(acc)
    return jnp.concatenate(halves, axis=0)


def lay_out(total, count):
    edge = count * NV
    z0 = jnp.concatenate([total[:NC]] * 16, axis=0)
    z1 = jnp.concatenate([total[NC:]] * 16, axis=0)
    shape = z0.shape
    row, col = iota(shape, 0), iota(shape, 1)
    y0 = col < edge
    z = jnp.where(row < 64, jnp.where(y0, z0, -z1), jnp.where(y0, z1, z0))
    z = jnp.where((row % 64) // NC == col % NV, z, 0.0)
    high = z.astype(jnp.bfloat16)
    low = (z - high.astype(jnp.float32)).astype(jnp.bfloat16)
    krow, kcol = iota((8, shape[1]), 0), iota((8, shape[1]), 1)
    pick = (jnp.where(kcol < edge, kcol, kcol - edge) // NV == krow).astype(jnp.bfloat16)
    return dot_nt(pick, high) + dot_nt(pick, low)


def kernel(
    count, scale_d, scale_x,
    piece_ref, hay_ref, weight_ref, map_ref, coul_ref, out_ref,
    vbuf, cbuf, hbuf, wbuf, sel, fbuf, spread, stage, res, xbuf, ybuf,
    load_sem, recv_sem, send_own, send_rel, send_res, recv_res, send_x, recv_x, send_y, recv_y,
):
    grp = lax.axis_index("grp")
    me = lax.axis_index("blk")
    p = lax.axis_index("pair")
    blocks = lax.axis_size("blk")
    dev = me * 2 + p
    planes = weight_ref.shape[1]
    edge = count * NV
    hub = HUB[0] * 2 + HUB[1]
    worker = me < STOPS + 1

    barrier = pltpu.get_barrier_semaphore()
    to = edges()
    expect = [0] * 16
    for (blk, core), senders in to.items():
        for sender in senders:
            expect[sender[0] * 2 + sender[1]] += 1

        @pl.when(dev == blk * 2 + core)
        def _():
            for sender in sorted(senders):
                pl.semaphore_signal(
                    barrier, inc=1, device_id=(grp, sender[0], sender[1]), device_id_type=MESH
                )

    load = pltpu.make_async_copy(weight_ref.at[0], wbuf, load_sem)

    @pl.when(worker)
    def _():
        load.start()

    hbuf[me, :count] = hay_ref[...]
    hbuf[me, count:] = jnp.zeros((8 - count, 128), jnp.float32)
    pl.semaphore_wait(barrier, lut(dev, expect))

    def own_copy(kind, slot):
        targets = [(OWN[m] + (None,) * 3)[slot] for m in range(8)]
        code = lut(me, [0 if t is None else t[0] * 2 + t[1] + 1 for t in targets])
        target = jnp.maximum(code - 1, 0)
        src, dst = ((piece_ref.at[0], vbuf), (piece_ref.at[1], cbuf), (hbuf.at[me], hbuf))[kind]
        return code > 0, pltpu.make_async_remote_copy(
            src_ref=src,
            dst_ref=dst.at[me],
            send_sem=send_own.at[kind, slot],
            recv_sem=recv_sem.at[kind, me],
            device_id=(grp, target // 2, target % 2),
            device_id_type=MESH,
        )

    def own_copies(act):
        for slot in range(3):
            for kind, core in ((2, 0), (0, 0), (1, 1)):
                go, copy = own_copy(kind, slot)

                @pl.when(go & (p == core))
                def _():
                    act(copy)

    own_copies(lambda copy: copy.start())

    vbuf[me] = piece_ref[0]
    cbuf[me] = piece_ref[1]
    spread[...] = spread_matrix(edge)
    mix = make_mix(hbuf[me], spread[...], count)
    amp = dot_nn(mix, piece_ref[0])
    cond_own = piece_ref[1].astype(jnp.float32)
    c_re, c_im = cond_own[:edge], cond_own[edge:]
    a_re, a_im = amp[:edge], amp[edge:]
    xbuf[dev, 0:1, :] = jnp.sum(c_re * a_re + c_im * a_im, axis=0, keepdims=True)
    xbuf[dev, 1:2, :] = jnp.sum(c_re * a_im - c_im * a_re, axis=0, keepdims=True)

    x_copy = pltpu.make_async_remote_copy(
        src_ref=xbuf.at[dev],
        dst_ref=xbuf.at[dev],
        send_sem=send_x,
        recv_sem=recv_x.at[dev],
        device_id=(grp, HUB[0], HUB[1]),
        device_id_type=MESH,
    )

    def y_copy(other):
        return pltpu.make_async_remote_copy(
            src_ref=ybuf,
            dst_ref=ybuf,
            send_sem=send_y.at[other],
            recv_sem=recv_y,
            device_id=(grp, other // 2, other % 2),
            device_id_type=MESH,
        )

    @pl.when(dev != hub)
    def _():
        x_copy.start()

    def whole(kind, b):
        return (vbuf.at[b], cbuf.at[b], hbuf.at[b])[kind]

    def relay(kind, b, target):
        return pltpu.make_async_remote_copy(
            src_ref=whole(kind, b),
            dst_ref=whole(kind, b),
            send_sem=send_rel.at[kind, b],
            recv_sem=recv_sem.at[kind, b],
            device_id=(grp, target // 2, target % 2),
            device_id_type=MESH,
        )

    def res_copy(t, b, s, core):
        return pltpu.make_async_remote_copy(
            src_ref=stage.at[t],
            dst_ref=res.at[s],
            send_sem=send_res.at[t, core],
            recv_sem=recv_res.at[s],
            device_id=(grp, b, core),
            device_id_type=MESH,
        )

    def unit_of(t):
        at = dev * 4 + t
        partner = [0] * 24
        for (s, core), units in UNITS.items():
            for step, (i, _) in enumerate(units):
                partner[(s * 2 + core) * 4 + step] = i
        i = lut(at, partner)
        return i, (i + me) % blocks

    def action_of(t, n):
        codes = [0] * 24
        for (s, core), units in UNITS.items():
            for step, (_, actions) in enumerate(units):
                if n < len(actions):
                    b, target = actions[n]
                    onward = 0 if target is None else target[0] * 2 + target[1] + 1
                    codes[(s * 2 + core) * 4 + step] = 1 + b + 8 * onward
        code = lut(dev * 4 + t, codes)
        packed = jnp.maximum(code - 1, 0)
        return code > 0, packed % 8, packed // 8

    @pl.when(worker)
    def _():
        sel[...] = jnp.where(
            map_ref[pl.ds(me, 1), :] == iota((planes, planes), 0), 1.0, 0.0
        ).astype(jnp.bfloat16)
        load.wait()

        def step(t, carry):
            @pl.when((dev == hub) & (t == 1))
            def _():
                for d in range(16):
                    if d != hub:
                        pltpu.make_async_copy(xbuf.at[d], xbuf.at[d], recv_x.at[d]).wait()
                ybuf[...] = jnp.sum(xbuf[...], axis=0) * coul_ref[...] * (0.5 * scale_x)
                for d in range(16):
                    if d != hub:
                        y_copy(d).start()

            for n in range(ACTIONS):
                go, b, onward = action_of(t, n)

                @pl.when(go)
                def _():
                    for kind in (2, 0, 1):
                        pltpu.make_async_copy(whole(kind, b), whole(kind, b), recv_sem.at[kind, b]).wait()

                        @pl.when(onward > 0)
                        def _():
                            relay(kind, b, jnp.maximum(onward - 1, 0)).start()

            i, b = unit_of(t)
            mix_i = make_mix(hbuf[i], spread[...], count)
            amp_i = dot_nn(mix_i, vbuf[i]).astype(jnp.bfloat16)
            perm = dot_nn(jnp.concatenate([amp_i, cbuf[i]], axis=0), sel[...])
            cond_t = perm[2 * edge :].T.astype(jnp.bfloat16)
            turned = jnp.concatenate([perm[edge : 2 * edge], -perm[:edge]], axis=0)
            both = jnp.concatenate([perm[: 2 * edge], turned], axis=1).astype(jnp.bfloat16)
            val_b = vbuf[b]
            swapped = jnp.concatenate([-val_b[edge:], val_b[:edge]], axis=0)
            v_lanes = jnp.concatenate(
                [
                    jnp.concatenate([val_b[:edge], swapped[:edge]], axis=0),
                    jnp.concatenate([val_b[edge:], swapped[edge:]], axis=0),
                ],
                axis=1,
            )
            tile = 256
            for r in range(planes // tile):
                rows = slice(r * tile, (r + 1) * tile)
                w = wbuf[rows, :].astype(jnp.float32)
                h = (dot_nn(cond_t[rows], both) * jnp.concatenate([w, w], axis=1)).astype(jnp.bfloat16)
                fbuf[rows, :] = dot_nt(h, v_lanes).astype(jnp.bfloat16)
            part = fold_block(dot_nn(cbuf[b], fbuf[...]), count) * scale_d
            stage[t, :, : 2 * edge] = part
            for core in range(2):
                mine = (b == me) & (p == core)

                @pl.when(mine)
                def _():
                    res[me, :, : 2 * edge] = part

                @pl.when(jnp.logical_not(mine))
                def _():
                    res_copy(t, b, me, core).start()

            return carry

        lax.fori_loop(0, 4, step, 0)

    @pl.when(dev != hub)
    def _():
        pltpu.make_async_copy(ybuf, ybuf, recv_y).wait()

    y_re, y_im = ybuf[0:1, :], ybuf[1:2, :]
    v_re = piece_ref[0, :edge].astype(jnp.float32)
    v_im = piece_ref[0, edge:].astype(jnp.float32)
    f_rows = jnp.concatenate([y_re * v_re + y_im * v_im, y_im * v_re - y_re * v_im], axis=0)
    total = fold_block(dot_nt(piece_ref[1], f_rows.astype(jnp.bfloat16)), count)

    for s in range(STOPS + 1):
        @pl.when(jnp.logical_not((me == s) & (p == 0)))
        def _():
            pltpu.make_async_copy(res.at[s], res.at[s], recv_res.at[s]).wait()
    for s in range(STOPS + 1):
        total = total + res[s, :, : 2 * edge]
    out_ref[...] = lay_out(total, count)[:count]

    own_copies(lambda copy: copy.wait_send())

    @pl.when(dev != hub)
    def _():
        x_copy.wait_send()

    @pl.when(dev == hub)
    def _():
        for d in range(16):
            if d != hub:
                y_copy(d).wait_send()

    @pl.when(worker)
    def _():
        def drain(t, carry):
            for n in range(ACTIONS):
                go, b, onward = action_of(t, n)

                @pl.when(go & (onward > 0))
                def _():
                    for kind in range(3):
                        relay(kind, b, jnp.maximum(onward - 1, 0)).wait_send()
            _, b = unit_of(t)
            for core in range(2):
                @pl.when(jnp.logical_not((b == me) & (p == core)))
                def _():
                    res_copy(t, b, me, core).wait_send()
            return carry

        lax.fori_loop(0, 4, drain, 0)


def scales(planes, count, total_k):
    return (
        -1.0 / (8.0 * math.sqrt(planes * count * (STOPS + 1))),
        1.0 / (8.0 * math.sqrt(planes * total_k)),
    )


def rows_of(wave):
    count, _, _, planes = wave.shape
    rows = wave.reshape(count, 2, NV, 2, planes).transpose(1, 3, 0, 2, 4)
    return rows.reshape(2, 2 * count * NV, planes)


def per_device(wavefunc, haydock, screened, coulomb, umklapp_map):
    count, _, _, planes = wavefunc.shape
    blocks = lax.axis_size("blk")
    edge = count * NV
    scale_d, scale_x = scales(planes, count, count * blocks)
    vmem = pl.BlockSpec(memory_space=pltpu.VMEM)
    dma = pltpu.SemaphoreType.DMA
    return pl.pallas_call(
        functools.partial(kernel, count, scale_d, scale_x),
        out_shape=jax.ShapeDtypeStruct((count, 128), jnp.float32),
        in_specs=[vmem, vmem, pl.BlockSpec(memory_space=pl.ANY), vmem, vmem],
        out_specs=vmem,
        scratch_shapes=[
            pltpu.VMEM((blocks, 2 * edge, planes), jnp.bfloat16),
            pltpu.VMEM((blocks, 2 * edge, planes), jnp.bfloat16),
            pltpu.VMEM((blocks, 8, 128), jnp.float32),
            pltpu.VMEM((planes, planes), jnp.bfloat16),
            pltpu.VMEM((planes, planes), jnp.bfloat16),
            pltpu.VMEM((planes, 2 * edge), jnp.bfloat16),
            pltpu.VMEM((128, 256), jnp.bfloat16),
            pltpu.VMEM((4, 2 * NV, 128), jnp.float32),
            pltpu.VMEM((STOPS + 1, 2 * NV, 128), jnp.float32),
            pltpu.VMEM((2 * blocks, 2, planes), jnp.float32),
            pltpu.VMEM((2, planes), jnp.float32),
            dma,
            dma((3, blocks)),
            dma((3, 3)),
            dma((3, blocks)),
            dma((4, 2)),
            dma((STOPS + 1,)),
            dma,
            dma((2 * blocks,)),
            dma((2 * blocks,)),
            dma,
        ],
        compiler_params=pltpu.CompilerParams(
            collective_id=0, has_side_effects=True, vmem_limit_bytes=40 * 1024 * 1024
        ),
    )(rows_of(wavefunc), haydock, screened, umklapp_map, coulomb.reshape(1, planes))


def make_pieces(wave, hay):
    count, bands, _, planes = wave.shape
    rows = wave.reshape(count, 2, NV, 2, planes).transpose(1, 3, 0, 2, 4)
    rows = rows.reshape(2, 2 * count * NV, planes)
    psi = hay.reshape(count, 2, NV, NC).transpose(1, 0, 3, 2)
    eye = jnp.eye(count, dtype=jnp.float32)
    wide = (psi[:, :, :, None, :] * eye[None, :, None, :, None]).reshape(2, count * NC, count * NV)
    top = jnp.concatenate([wide[0], -wide[1]], axis=1)
    low = jnp.concatenate([wide[1], wide[0]], axis=1)
    mix = jnp.concatenate([top, low], axis=0).astype(jnp.bfloat16)
    return rows, mix


def unpack_result(total, count):
    half = count * NC
    out_re = total[:NV, :half] - total[NV:, half : 2 * half]
    out_im = total[NV:, :half] + total[:NV, half : 2 * half]
    out = jnp.stack([out_re, out_im]).reshape(2, NV, count, NC)
    return out.transpose(2, 0, 1, 3).reshape(count, 2 * NV * NC)


def fold_rows(f_rows, cond, count):
    t = dot_nt(f_rows, cond)
    rows, lanes = t.shape
    keep = (lax.broadcasted_iota(jnp.int32, t.shape, 0) // NV) % count == (
        lax.broadcasted_iota(jnp.int32, t.shape, 1) // NC
    ) % count
    t = jnp.where(keep, t, 0.0).reshape(2, count, NV, lanes)
    return jnp.sum(t, axis=1).reshape(2 * NV, lanes)


def per_device_general(wavefunc, haydock, screened, coulomb, umklapp_map):
    count, _, _, planes = wavefunc.shape
    blocks = lax.axis_size("blk")
    edge = count * NV
    rows, mix = make_pieces(wavefunc, haydock)
    val, cond = rows[0], rows[1]
    amp = dot_nn(mix, val)
    wide = cond.astype(jnp.float32)
    c_re, c_im, a_re, a_im = wide[:edge], wide[edge:], amp[:edge], amp[edge:]
    x_re = jnp.sum(c_re * a_re + c_im * a_im, axis=0)
    x_im = jnp.sum(c_re * a_im - c_im * a_re, axis=0)
    xs = lax.psum(jnp.stack([x_re, x_im]), "blk")
    scale_d, scale_x = scales(planes, count, count * blocks)
    y = xs * coulomb * scale_x
    v_re, v_im = val[:edge].astype(jnp.float32), val[edge:].astype(jnp.float32)
    f = jnp.concatenate([y[0] * v_re + y[1] * v_im, y[1] * v_re - y[0] * v_im], axis=0)
    current = jnp.concatenate([amp.astype(jnp.bfloat16), cond], axis=0)
    for stop in range(STOPS + 1):
        if stop > 0:
            current = lax.ppermute(current, "blk", [(i, (i + 1) % blocks) for i in range(blocks)])
        held = lax.axis_index("blk") == stop
        weight = lax.psum(jnp.where(held, screened[0], jnp.zeros_like(screened[0])), "blk")
        pick = (umklapp_map[stop][:, None] == jnp.arange(planes)[None, :]).astype(jnp.bfloat16)
        perm = dot_nt(current, pick).astype(jnp.bfloat16)
        amp_p, cond_t = perm[: 2 * edge], perm[2 * edge :].T
        turned = jnp.concatenate([amp_p[edge:], -amp_p[:edge]], axis=0)
        h_re = (dot_nn(cond_t, amp_p) * weight.astype(jnp.float32)).astype(jnp.bfloat16)
        h_im = (dot_nn(cond_t, turned) * weight.astype(jnp.float32)).astype(jnp.bfloat16)
        g_re, g_im = dot_nt(val, h_re), dot_nt(val, h_im)
        f = f + scale_d * jnp.concatenate([g_re[:edge] + g_im[edge:], g_im[:edge] - g_re[edge:]], axis=0)
    return unpack_result(fold_rows(f.astype(jnp.bfloat16), cond, count), count)


def solution(mesh):
    placed = (
        P(("grp", "blk"), None, None, None),
        P(("grp", "blk"), None),
        P(("grp", "blk"), None, None),
        P("grp"),
        P(),
    )
    body = per_device if mesh.shape["blk"] == 8 and mesh.shape["pair"] == 2 else per_device_general
    return jax.shard_map(
        body, mesh=mesh, in_specs=placed, out_specs=P(("grp", "blk"), None), check_vma=False
    )
```

time: 42.6 us -> 35.4 us (0.83)
  the two profiles are of different devices: /device:TPU:0 before, /device:TPU:27 now
where the time goes in v1:
time: 35.4 us; the launch traced here: 35.1 us
  Pallas kernels  30.1 us (85%)
  local copies, waits for them, and re-layouts  4.93 us (14%)
    pallas_call x1, Pallas kernels, per_device(): pl.pallas_call(functools.partial(kernel, count, scale_d, scale_x), out_sh...  30.1 us
    unnamed x7, local copies, waits for them, and re-layouts  3.25 us
    reshape x1, local copies, waits for them, and re-layouts, rows_of(): rows = wave.reshape(count, 2, NV, 2, planes).transpose(1, 3, 0, 2, 4)  0.99 us

profile of v1, /device:TPU:27, one launch (start us, length us, event | category | flops | bytes accessed | tf_op | source)
XLA Modules:
  0.0 35.1 jit_solution(950688169295033603)
XLA Ops:
  0.0 0.7 %reshape.11.coul_ref = f32[1,768]{1,0:T(1,128)S(1)} reshape(f32[768]{0:T(1024)} %param.8) | data formatting | bytes 6144 | tf_op jit(solution)/shard_map/reshape | solution.py:449
  0.7 1.0 %copy.6 = bf16[6,2,8,2,768]{4,2,0,3,1:T(8,128)(2,1)S(1)} copy(bf16[6,2,8,2,768]{4,3,2,1,0:T(2,128)(2,1)} %bitcast.5) | data formatting | bytes 589824 | tf_op jit(solution)/shard_map/reshape | solution.py:407
  1.7 0.0 copy-start
  1.7 1.3 %copy-done = bf16[1,768,768]{2,1,0:T(8,128)(2,1)S(1)} copy-done((bf16[1,768,768]{2,1,0:T(8,128)(2,1)S(1)}, bf16[1,768,768]{2,1,0:T(8,128)(2,1)}, u32[]{:S(2)}) %copy-start) | copy-done | bytes 1179672
  3.0 0.0 copy-start.1
  3.0 0.7 %copy-done.1 = s32[3,768]{1,0:T(4,128)S(1)} copy-done((s32[3,768]{1,0:T(4,128)S(1)}, s32[3,768]{1,0:T(4,128)}, u32[]{:S(2)}) %copy-start.1) | copy-done | bytes 9240
  3.7 0.0 copy-start.2
  3.7 0.7 %copy-done.2 = f32[6,128]{1,0:T(8,128)S(1)} copy-done((f32[6,128]{1,0:T(8,128)S(1)}, f32[6,128]{1,0:T(8,128)}, u32[]{:S(2)}) %copy-start.2) | copy-done | bytes 3096
  4.4 30.1 %shard_map.55 = f32[6,128]{1,0:T(8,128)S(1)} custom-call(bf16[2,96,768]{2,1,0:T(8,128)(2,1)S(1)} %bitcast.4, f32[6,128]{1,0:T(8,128)S(1)} %copy-done.2, bf16[1,768,768]{2,1,0:T(8,128)(2,1)S(1)} %copy-done, s32[3,768]{1,0:T(4,128)S(1)} %copy-done.1, f32[1,768]{1,0:T(1,128)S(1)} %reshape.11.coul_ref), custom_call_target="tpu_custom_call" | custom-call | tf_op jit(solution)/shard_map/pallas_call | solution.py:418
  34.5 0.6 %copy.8 = f32[6,128]{1,0:T(8,128)} copy(f32[6,128]{1,0:T(8,128)S(1)} %shard_map.55) | data formatting | bytes 6144
Async XLA Ops:
  1.7 1.3 %copy-start = (bf16[1,768,768]{2,1,0:T(8,128)(2,1)S(1)}, bf16[1,768,768]{2,1,0:T(8,128)(2,1)}, u32[]{:S(2)}) copy-start(bf16[1,768,768]{2,1,0:T(8,128)(2,1)} %weight_ref.1) | copy-start | bytes 3538948
  3.0 0.7 %copy-start.1 = (s32[3,768]{1,0:T(4,128)S(1)}, s32[3,768]{1,0:T(4,128)}, u32[]{:S(2)}) copy-start(s32[3,768]{1,0:T(4,128)} %map_ref.1) | copy-start | bytes 27652
  3.7 0.7 %copy-start.2 = (f32[6,128]{1,0:T(8,128)S(1)}, f32[6,128]{1,0:T(8,128)}, u32[]{:S(2)}) copy-start(f32[6,128]{1,0:T(8,128)} %hay_ref.1) | copy-start | bytes 9220

commit v2 on v1

v2 whole, which is shorter than its diff:
```python
import functools
import math

import jax
import jax.numpy as jnp
from jax import lax
from jax.experimental import pallas as pl
from jax.experimental.pallas import tpu as pltpu
from jax.sharding import PartitionSpec as P

NV = 8
NC = 8
STOPS = 2
MESH = pl.DeviceIdType.MESH
NT = (((1,), (1,)), ((), ()))

OWN = {
    0: ((1, 0), (1, 1), (2, 0)),
    1: ((0, 1), (2, 1)),
    2: ((0, 0),),
    3: ((1, 0), (2, 1)),
    4: ((2, 0),),
    5: ((3, 0),),
    6: ((2, 0),),
    7: ((3, 1),),
}
ROUTE = {(3, 0): (5, ((1, 1), (2, 1))), (3, 1): (7, ((1, 1), (2, 1)))}
UNITS = {
    (0, 0): ((0, ()), (2, ((2, (1, 0)),)), (4, ((4, (1, 1)),)), (6, ((6, (1, 1)),))),
    (0, 1): ((1, ((1, None),)), (3, ((3, None),)), (5, ((5, None),)), (7, ((7, None),))),
    (1, 0): ((0, ((0, None),)), (1, ((3, (0, 1)), (2, None))), (2, ()), (3, ((4, None),))),
    (1, 1): ((7, ((0, None), (5, (0, 1)), (7, (0, 1)))), (4, ((4, (1, 0)),)), (5, ((6, None),)), (6, ())),
    (2, 0): ((0, ((0, None),)), (2, ((4, (0, 0)),)), (6, ((6, (0, 0)),)), (4, ())),
    (2, 1): ((1, ((1, None), (3, None))), (3, ((5, None),)), (7, ((7, None),)), (5, ())),
}
HUB = (0, 1)
ACTIONS = 3
CHUNKS = 2


def edges():
    to = {}
    for blk, targets in OWN.items():
        for target in targets:
            for core in range(2):
                to.setdefault(target, set()).add((blk, core))
    for worker, units in UNITS.items():
        for _, actions in units:
            for _, target in actions:
                if target is not None:
                    to.setdefault(target, set()).add(worker)
    for router, (_, targets) in ROUTE.items():
        for target in targets:
            to.setdefault(target, set()).add(router)
    for blk in range(8):
        for core in range(2):
            if (blk, core) != HUB:
                to.setdefault(HUB, set()).add((blk, core))
    for blk in range(STOPS + 1):
        to.setdefault((blk, 1), set()).add((blk, 0))
    return to


def dot_nt(a, b):
    return lax.dot_general(a, b, NT, preferred_element_type=jnp.float32)


def dot_nn(a, b):
    return jnp.dot(a, b, preferred_element_type=jnp.float32)


def lut(index, values):
    out = jnp.int32(0)
    for n, value in enumerate(values):
        if value:
            out = jnp.where(index == n, jnp.int32(value), out)
    return out


def iota(shape, dim):
    return lax.broadcasted_iota(jnp.int32, shape, dim)


def spread_matrix(edge):
    half = edge
    row, col = iota((128, 256), 0), iota((128, 256), 1)
    lane = col % 128
    y = (lane >= half).astype(jnp.int32)
    part = jnp.where(col >= 128, 1 - y, y)
    return ((row // 64 == part) & ((row % 64) // NC == lane % NV)).astype(jnp.bfloat16)


def make_mix(hay, spread, count):
    edge = count * NV
    tall = jnp.concatenate(
        [jnp.broadcast_to(hay[k : k + 1, :], (NC, 128)) for _ in range(2) for k in range(count)], axis=0
    )
    shape = (2 * edge, 128)
    row, col = iota(shape, 0), iota(shape, 1)
    tall = jnp.where(row % NC == col % NC, tall, 0.0).astype(jnp.bfloat16)
    q = dot_nn(tall, spread)
    top = row < edge
    k_row = jnp.where(top, row, row - edge) // NC
    k_col = jnp.where(col < edge, col, col - edge) // NV
    mix = jnp.where(top, jnp.where(col < edge, q[:, :128], -q[:, :128]), q[:, 128:])
    keep = (k_row == k_col) & (col < 2 * edge)
    return jnp.where(keep, mix, 0.0).astype(jnp.bfloat16)[:, : 2 * edge]


def fold_block(t, count):
    edge = count * NV
    row, col = iota(t.shape, 0), iota(t.shape, 1)
    k_row = jnp.where(row < edge, row, row - edge) // NC
    k_col = jnp.where(col < edge, col, col - edge) // NV
    t = jnp.where(k_row == k_col, t, 0.0)
    halves = []
    for x in range(2):
        acc = t[x * edge : x * edge + NC]
        for k in range(1, count):
            acc = acc + t[x * edge + k * NC : x * edge + (k + 1) * NC]
        halves.append(acc)
    return jnp.concatenate(halves, axis=0)


def lay_out(total, count):
    edge = count * NV
    z0 = jnp.concatenate([total[:NC]] * 16, axis=0)
    z1 = jnp.concatenate([total[NC:]] * 16, axis=0)
    shape = z0.shape
    row, col = iota(shape, 0), iota(shape, 1)
    y0 = col < edge
    z = jnp.where(row < 64, jnp.where(y0, z0, -z1), jnp.where(y0, z1, z0))
    z = jnp.where((row % 64) // NC == col % NV, z, 0.0)
    high = z.astype(jnp.bfloat16)
    low = (z - high.astype(jnp.float32)).astype(jnp.bfloat16)
    krow, kcol = iota((8, shape[1]), 0), iota((8, shape[1]), 1)
    pick = (jnp.where(kcol < edge, kcol, kcol - edge) // NV == krow).astype(jnp.bfloat16)
    return dot_nt(pick, high) + dot_nt(pick, low)


def kernel(
    count, scale_d, scale_x,
    piece_ref, hay_ref, weight_ref, map_ref, coul_ref, out_ref,
    pbuf, hbuf, wbuf, mbuf, coul, sel, fbuf, spread, stage, res, xbuf, ybuf,
    load_sem, recv_sem, recv_hay, send_sem, send_hay, send_res, recv_res, send_x, recv_x, send_y, recv_y,
):
    grp = lax.axis_index("grp")
    me = lax.axis_index("blk")
    p = lax.axis_index("pair")
    blocks = lax.axis_size("blk")
    dev = me * 2 + p
    planes = weight_ref.shape[1]
    edge = count * NV
    hub = HUB[0] * 2 + HUB[1]
    worker = me < STOPS + 1
    chunk = 2 * edge // CHUNKS

    def each(n, body):
        def wrapped(i, carry):
            body(i)
            return carry

        lax.fori_loop(0, n, wrapped, 0)

    barrier = pltpu.get_barrier_semaphore()
    to = edges()
    expect = [0] * 16
    masks = [0] * 16
    for (blk, core), senders in to.items():
        for sender in senders:
            expect[sender[0] * 2 + sender[1]] += 1
            masks[sender[0] * 2 + sender[1]] |= 1 << (blk * 2 + core)

    def greet(other):
        mask = lut(other, masks)
        power = lut(dev, [1 << d for d in range(8)])

        @pl.when((power > 0) & (mask // jnp.maximum(power, 1) % 2 == 1))
        def _():
            pl.semaphore_signal(barrier, inc=1, device_id=(grp, other // 2, other % 2), device_id_type=MESH)

    each(16, greet)

    loads = [
        pltpu.make_async_copy(src, dst, load_sem.at[n])
        for n, (src, dst) in enumerate(
            (
                (hay_ref, hbuf.at[me, pl.ds(0, count)]),
                (piece_ref, pbuf.at[me]),
                (map_ref, mbuf),
                (coul_ref, coul),
                (weight_ref.at[0], wbuf),
            )
        )
    ]
    for load in loads[:4]:
        load.start()

    @pl.when(worker)
    def _():
        loads[4].start()

    pl.semaphore_wait(barrier, lut(dev, expect))

    def rows_at(c):
        return pl.ds(pl.multiple_of(c * chunk, chunk), chunk)

    def hay_at(b):
        return hbuf.at[b, pl.ds(0, count)]

    def remote(src, dst, send, recv, target):
        return pltpu.make_async_remote_copy(
            src_ref=src, dst_ref=dst, send_sem=send, recv_sem=recv,
            device_id=(grp, target // 2, target % 2), device_id_type=MESH,
        )

    def drained(n, most, ref_of, sem):
        for m in range(1, most + 1):
            @pl.when(n == m)
            def _():
                pltpu.make_async_copy(ref_of(m), ref_of(m), sem).wait()

    own_targets = [0] * 24
    for m, targets in OWN.items():
        for slot, (blk, core) in enumerate(targets):
            own_targets[m * 3 + slot] = blk * 2 + core + 1

    def own_slot(slot):
        code = lut(me * 3 + slot, own_targets)
        target = jnp.maximum(code - 1, 0)

        @pl.when(code > 0)
        def _():
            @pl.when(p == 0)
            def _():
                remote(hay_ref, hay_at(me), send_hay.at[0], recv_hay.at[me], target).start()

            each(CHUNKS, lambda c: remote(
                piece_ref.at[p, rows_at(c)], pbuf.at[me, p, rows_at(c)],
                send_sem.at[0], recv_sem.at[me, c], target,
            ).start())

    each(3, own_slot)

    spread[...] = spread_matrix(edge)
    for load in loads[:4]:
        load.wait()
    mix = make_mix(hbuf[me, :count], spread[...], count)
    amp = dot_nn(mix, pbuf[me, 0])
    cond_own = pbuf[me, 1].astype(jnp.float32)
    c_re, c_im = cond_own[:edge], cond_own[edge:]
    a_re, a_im = amp[:edge], amp[edge:]
    xbuf[dev, 0:1, :] = jnp.sum(c_re * a_re + c_im * a_im, axis=0, keepdims=True)
    xbuf[dev, 1:2, :] = jnp.sum(c_re * a_im - c_im * a_re, axis=0, keepdims=True)
    x_copy = remote(xbuf.at[dev], xbuf.at[dev], send_x, recv_x, jnp.int32(hub))

    def others(body):
        def guarded(d):
            @pl.when(d != hub)
            def _():
                body(d)

        each(16, guarded)

    def y_copy(other):
        return remote(ybuf, ybuf, send_y, recv_y, other)

    @pl.when(dev != hub)
    def _():
        x_copy.start()

    def arrive(b, pass_on):
        pltpu.make_async_copy(hay_at(b), hay_at(b), recv_hay.at[b]).wait()
        pass_on(lambda target: remote(hay_at(b), hay_at(b), send_hay.at[1], recv_hay.at[b], target).start())

        def per_chunk(c):
            ref = pbuf.at[b, :, rows_at(c)]
            pltpu.make_async_copy(ref, ref, recv_sem.at[b, c]).wait()
            pass_on(lambda target: remote(ref, ref, send_sem.at[1], recv_sem.at[b, c], target).start())

        each(CHUNKS, per_chunk)

    def res_copy(t, b, core):
        return remote(stage.at[t], res.at[me], send_res, recv_res, b * 2 + core)

    partners = [0] * 24
    codes = [0] * (24 * ACTIONS)
    for (s, core), units in UNITS.items():
        for t, (i, actions) in enumerate(units):
            at = (s * 2 + core) * 4 + t
            partners[at] = i
            for n, (b, target) in enumerate(actions):
                onward = 0 if target is None else target[0] * 2 + target[1] + 1
                codes[at * ACTIONS + n] = 1 + b + 8 * onward

    def unit_of(t):
        i = lut(dev * 4 + t, partners)
        return i, (i + me) % blocks

    def action_of(t, n):
        code = lut((dev * 4 + t) * ACTIONS + n, codes)
        packed = jnp.maximum(code - 1, 0)
        onward = packed // 8
        return code > 0, packed % 8, onward > 0, jnp.maximum(onward - 1, 0)

    fifteen = xbuf.at[pl.ds(0, 15)]

    @pl.when(worker)
    def _():
        sel[...] = jnp.where(
            mbuf[pl.ds(me, 1), :] == iota((planes, planes), 0), 1.0, 0.0
        ).astype(jnp.bfloat16)
        loads[4].wait()

        def step(t):
            @pl.when((dev == hub) & (t == 1))
            def _():
                pltpu.make_async_copy(fifteen, fifteen, recv_x).wait()
                coul_row = jnp.concatenate([coul[n : n + 1, :] for n in range(planes // 128)], axis=1)
                ybuf[...] = jnp.sum(xbuf[...], axis=0) * coul_row * (0.5 * scale_x)
                others(lambda d: y_copy(d).start())

            def act(n):
                go, b, onward, target = action_of(t, n)

                def pass_on(start):
                    @pl.when(onward)
                    def _():
                        start(target)

                @pl.when(go)
                def _():
                    arrive(b, pass_on)

            each(ACTIONS, act)
            i, b = unit_of(t)
            mix_i = make_mix(hbuf[i, :count], spread[...], count)
            amp_i = dot_nn(mix_i, pbuf[i, 0]).astype(jnp.bfloat16)
            perm = dot_nn(jnp.concatenate([amp_i, pbuf[i, 1]], axis=0), sel[...])
            cond_t = perm[2 * edge :].T.astype(jnp.bfloat16)
            turned = jnp.concatenate([perm[edge : 2 * edge], -perm[:edge]], axis=0)
            both = jnp.concatenate([perm[: 2 * edge], turned], axis=1).astype(jnp.bfloat16)
            val_b = pbuf[b, 0]
            swapped = jnp.concatenate([-val_b[edge:], val_b[:edge]], axis=0)
            v_lanes = jnp.concatenate(
                [
                    jnp.concatenate([val_b[:edge], swapped[:edge]], axis=0),
                    jnp.concatenate([val_b[edge:], swapped[edge:]], axis=0),
                ],
                axis=1,
            )
            tile = 256
            for r in range(planes // tile):
                rows = slice(r * tile, (r + 1) * tile)
                w = wbuf[rows, :].astype(jnp.float32)
                h = (dot_nn(cond_t[rows], both) * jnp.concatenate([w, w], axis=1)).astype(jnp.bfloat16)
                fbuf[rows, :] = dot_nt(h, v_lanes).astype(jnp.bfloat16)
            part = fold_block(dot_nn(pbuf[b, 1], fbuf[...]), count) * scale_d
            stage[t, :, : 2 * edge] = part

            @pl.when((b == me) & (p == 0))
            def _():
                res[me, :, : 2 * edge] = part


            def send_result(core):
                @pl.when(jnp.logical_not((b == me) & (p == core)))
                def _():
                    res_copy(t, b, core).start()

            each(2, send_result)

        each(4, step)

    routed = 5 + 2 * p

    @pl.when(me == 3)
    def _():
        arrive(routed, lambda start: each(2, lambda slot: start(3 + 2 * slot)))

    @pl.when(dev != hub)
    def _():
        pltpu.make_async_copy(ybuf, ybuf, recv_y).wait()

    y_re, y_im = ybuf[0:1, :], ybuf[1:2, :]
    v_re = pbuf[me, 0, :edge].astype(jnp.float32)
    v_im = pbuf[me, 0, edge:].astype(jnp.float32)
    f_rows = jnp.concatenate([y_re * v_re + y_im * v_im, y_im * v_re - y_re * v_im], axis=0)
    total = fold_block(dot_nt(pbuf[me, 1], f_rows.astype(jnp.bfloat16)), count)

    awaited = jnp.where((p == 0) & worker, STOPS, STOPS + 1)
    drained(awaited, STOPS + 1, lambda n: res.at[pl.ds(0, n)], recv_res)
    for s in range(STOPS + 1):
        total = total + res[s, :, : 2 * edge]
    out_ref[...] = lay_out(total, count)[:count]

    own_count = lut(me, [len(OWN[m]) for m in range(8)])
    drained(own_count, 3, lambda n: pbuf.at[pl.ds(0, n), 0], send_sem.at[0])
    drained(jnp.where(p == 0, own_count, 0), 3, lambda n: hbuf.at[pl.ds(0, n), pl.ds(0, count)], send_hay.at[0])
    passed = [0] * 16
    for (s, core), units in UNITS.items():
        passed[s * 2 + core] = sum(target is not None for _, actions in units for _, target in actions)
    for (blk, core), (_, targets) in ROUTE.items():
        passed[blk * 2 + core] = len(targets)
    passed = lut(dev, passed)
    drained(passed, 3, lambda n: pbuf.at[pl.ds(0, n)], send_sem.at[1])
    drained(passed, 3, lambda n: hbuf.at[pl.ds(0, n), pl.ds(0, count)], send_hay.at[1])

    @pl.when(dev != hub)
    def _():
        x_copy.wait_send()

    @pl.when(dev == hub)
    def _():
        pltpu.make_async_copy(fifteen, fifteen, send_y).wait()

    for n in (7, 8):
        @pl.when(worker & (8 - n == 1 - p))
        def _():
            pltpu.make_async_copy(stage.at[pl.ds(0, n)], stage.at[pl.ds(0, n)], send_res).wait()


def scales(planes, count, total_k):
    return (
        -1.0 / (8.0 * math.sqrt(planes * count * (STOPS + 1))),
        1.0 / (8.0 * math.sqrt(planes * total_k)),
    )


def rows_of(wave):
    count, _, _, planes = wave.shape
    rows = wave.reshape(count, 2, NV, 2, planes).transpose(1, 3, 0, 2, 4)
    return rows.reshape(2, 2 * count * NV, planes)


def per_device(wavefunc, haydock, screened, coulomb, umklapp_map):
    count, _, _, planes = wavefunc.shape
    blocks = lax.axis_size("blk")
    edge = count * NV
    scale_d, scale_x = scales(planes, count, count * blocks)
    dma = pltpu.SemaphoreType.DMA
    return pl.pallas_call(
        functools.partial(kernel, count, scale_d, scale_x),
        out_shape=jax.ShapeDtypeStruct((count, 128), jnp.float32),
        in_specs=[pl.BlockSpec(memory_space=pltpu.HBM)] * 5,
        out_specs=pl.BlockSpec(memory_space=pltpu.VMEM),
        scratch_shapes=[
            pltpu.VMEM((blocks, 2, 2 * edge, planes), jnp.bfloat16),
            pltpu.VMEM((blocks, 8, 128), jnp.float32),
            pltpu.VMEM((planes, planes), jnp.bfloat16),
            pltpu.VMEM((STOPS + 1, planes), jnp.int32),
            pltpu.VMEM((planes // 128, 128), jnp.float32),
            pltpu.VMEM((planes, planes), jnp.bfloat16),
            pltpu.VMEM((planes, 2 * edge), jnp.bfloat16),
            pltpu.VMEM((128, 256), jnp.bfloat16),
            pltpu.VMEM((8, 2 * NV, 128), jnp.float32),
            pltpu.VMEM((STOPS + 1, 2 * NV, 128), jnp.float32),
            pltpu.VMEM((2 * blocks, 2, planes), jnp.float32),
            pltpu.VMEM((2, planes), jnp.float32),
            dma((5,)),
            dma((blocks, CHUNKS)),
            dma((blocks,)),
            dma((2,)),
            dma((2,)),
            dma,
            dma,
            dma,
            dma,
            dma,
            dma,
        ],
        compiler_params=pltpu.CompilerParams(
            collective_id=0, has_side_effects=True, vmem_limit_bytes=62 * 1024 * 1024
        ),
    )(rows_of(wavefunc), haydock, screened, umklapp_map, coulomb.reshape(-1, 128))


def make_pieces(wave, hay):
    count, bands, _, planes = wave.shape
    rows = wave.reshape(count, 2, NV, 2, planes).transpose(1, 3, 0, 2, 4)
    rows = rows.reshape(2, 2 * count * NV, planes)
    psi = hay.reshape(count, 2, NV, NC).transpose(1, 0, 3, 2)
    eye = jnp.eye(count, dtype=jnp.float32)
    wide = (psi[:, :, :, None, :] * eye[None, :, None, :, None]).reshape(2, count * NC, count * NV)
    top = jnp.concatenate([wide[0], -wide[1]], axis=1)
    low = jnp.concatenate([wide[1], wide[0]], axis=1)
    mix = jnp.concatenate([top, low], axis=0).astype(jnp.bfloat16)
    return rows, mix


def unpack_result(total, count):
    half = count * NC
    out_re = total[:NV, :half] - total[NV:, half : 2 * half]
    out_im = total[NV:, :half] + total[:NV, half : 2 * half]
    out = jnp.stack([out_re, out_im]).reshape(2, NV, count, NC)
    return out.transpose(2, 0, 1, 3).reshape(count, 2 * NV * NC)


def fold_rows(f_rows, cond, count):
    t = dot_nt(f_rows, cond)
    rows, lanes = t.shape
    keep = (lax.broadcasted_iota(jnp.int32, t.shape, 0) // NV) % count == (
        lax.broadcasted_iota(jnp.int32, t.shape, 1) // NC
    ) % count
    t = jnp.where(keep, t, 0.0).reshape(2, count, NV, lanes)
    return jnp.sum(t, axis=1).reshape(2 * NV, lanes)


def per_device_general(wavefunc, haydock, screened, coulomb, umklapp_map):
    count, _, _, planes = wavefunc.shape
    blocks = lax.axis_size("blk")
    edge = count * NV
    rows, mix = make_pieces(wavefunc, haydock)
    val, cond = rows[0], rows[1]
    amp = dot_nn(mix, val)
    wide = cond.astype(jnp.float32)
    c_re, c_im, a_re, a_im = wide[:edge], wide[edge:], amp[:edge], amp[edge:]
    x_re = jnp.sum(c_re * a_re + c_im * a_im, axis=0)
    x_im = jnp.sum(c_re * a_im - c_im * a_re, axis=0)
    xs = lax.psum(jnp.stack([x_re, x_im]), "blk")
    scale_d, scale_x = scales(planes, count, count * blocks)
    y = xs * coulomb * scale_x
    v_re, v_im = val[:edge].astype(jnp.float32), val[edge:].astype(jnp.float32)
    f = jnp.concatenate([y[0] * v_re + y[1] * v_im, y[1] * v_re - y[0] * v_im], axis=0)
    current = jnp.concatenate([amp.astype(jnp.bfloat16), cond], axis=0)
    for stop in range(STOPS + 1):
        if stop > 0:
            current = lax.ppermute(current, "blk", [(i, (i + 1) % blocks) for i in range(blocks)])
        held = lax.axis_index("blk") == stop
        weight = lax.psum(jnp.where(held, screened[0], jnp.zeros_like(screened[0])), "blk")
        pick = (umklapp_map[stop][:, None] == jnp.arange(planes)[None, :]).astype(jnp.bfloat16)
        perm = dot_nt(current, pick).astype(jnp.bfloat16)
        amp_p, cond_t = perm[: 2 * edge], perm[2 * edge :].T
        turned = jnp.concatenate([amp_p[edge:], -amp_p[:edge]], axis=0)
        h_re = (dot_nn(cond_t, amp_p) * weight.astype(jnp.float32)).astype(jnp.bfloat16)
        h_im = (dot_nn(cond_t, turned) * weight.astype(jnp.float32)).astype(jnp.bfloat16)
        g_re, g_im = dot_nt(val, h_re), dot_nt(val, h_im)
        f = f + scale_d * jnp.concatenate([g_re[:edge] + g_im[edge:], g_im[:edge] - g_re[edge:]], axis=0)
    return unpack_result(fold_rows(f.astype(jnp.bfloat16), cond, count), count)


def solution(mesh):
    placed = (
        P(("grp", "blk"), None, None, None),
        P(("grp", "blk"), None),
        P(("grp", "blk"), None, None),
        P("grp"),
        P(),
    )
    body = per_device if mesh.shape["blk"] == 8 and mesh.shape["pair"] == 2 else per_device_general
    return jax.shard_map(
        body, mesh=mesh, in_specs=placed, out_specs=P(("grp", "blk"), None), check_vma=False
    )
```

time: 35.4 us -> 33.6 us (0.949)
  local copies, waits for them, and re-layouts: 4.93 us -> 2.97 us
  Pallas kernels: 30.1 us -> 30.5 us
    unnamed x7 -> x1, local copies, waits for them, and re-layouts: 3.25 us -> 1.28 us
    reshape x1, local copies, waits for them, and re-layouts: 0.99 us -> 1.7 us  [rows_of(): rows = wave.reshape(count, 2, NV, 2, planes).transpose(1, 3, 0, 2, 4)]
    reshape x1 -> x0, local copies, waits for them, and re-layouts: 0.69 us -> none  [per_device(): coulomb.reshape(1, planes)]
    pallas_call x1, Pallas kernels: 30.1 us -> 30.5 us  [per_device(): pl.pallas_call(functools.partial(kernel, count, scale_d, scale_x), out_sh...]
where the time goes in v2:
time: 33.6 us; the launch traced here: 33.4 us
  Pallas kernels  30.5 us (91%)
  local copies, waits for them, and re-layouts  2.97 us (9%)
    pallas_call x1, Pallas kernels, per_device(): pl.pallas_call(functools.partial(kernel, count, scale_d, scale_x), out_sh...  30.5 us
    reshape x1, local copies, waits for them, and re-layouts, rows_of(): rows = wave.reshape(count, 2, NV, 2, planes).transpose(1, 3, 0, 2, 4)  1.7 us
    unnamed x1, local copies, waits for them, and re-layouts  1.28 us

profile of v2, /device:TPU:27, one launch (start us, length us, event | category | flops | bytes accessed | tf_op | source)
XLA Modules:
  0.0 33.4 jit_solution(5332093675780428850)
XLA Ops:
  0.0 1.7 %copy.6 = bf16[6,2,8,2,768]{4,2,0,3,1:T(8,128)(2,1)} copy(bf16[6,2,8,2,768]{4,3,2,1,0:T(2,128)(2,1)} %bitcast.6) | data formatting | bytes 589824 | tf_op jit(solution)/shard_map/reshape | solution.py:432
  1.7 30.5 %shard_map.55 = f32[6,128]{1,0:T(8,128)} custom-call(bf16[2,96,768]{2,1,0:T(8,128)(2,1)} %bitcast.5, f32[6,128]{1,0:T(8,128)} %hay_ref.1, bf16[1,768,768]{2,1,0:T(8,128)(2,1)} %weight_ref.1, s32[3,768]{1,0:T(4,128)} %map_ref.1, f32[6,128]{1,0:T(8,128)} %bitcast.7), custom_call_target="tpu_custom_call" | custom-call | tf_op jit(solution)/shard_map/pallas_call | solution.py:442
  32.2 1.3 %copy.8 = f32[6,128]{1,0:T(8,128)} copy(f32[6,128]{1,0:T(8,128)} %shard_map.55) | data formatting | bytes 6144

commit v3 on v2

--- a/solution.py
+++ b/solution.py
@@ -15,24 +15,33 @@
 NT = (((1,), (1,)), ((), ()))
 
 OWN = {
-    0: ((1, 0), (1, 1), (2, 0)),
-    1: ((0, 1), (2, 1)),
+    0: ((1, 0), (2, 0)),
+    1: ((0, 1),),
     2: ((0, 0),),
-    3: ((1, 0), (2, 1)),
+    3: ((1, 1), (2, 1)),
     4: ((2, 0),),
     5: ((3, 0),),
     6: ((2, 0),),
     7: ((3, 1),),
 }
-ROUTE = {(3, 0): (5, ((1, 1), (2, 1))), (3, 1): (7, ((1, 1), (2, 1)))}
 UNITS = {
-    (0, 0): ((0, ()), (2, ((2, (1, 0)),)), (4, ((4, (1, 1)),)), (6, ((6, (1, 1)),))),
-    (0, 1): ((1, ((1, None),)), (3, ((3, None),)), (5, ((5, None),)), (7, ((7, None),))),
-    (1, 0): ((0, ((0, None),)), (1, ((3, (0, 1)), (2, None))), (2, ()), (3, ((4, None),))),
-    (1, 1): ((7, ((0, None), (5, (0, 1)), (7, (0, 1)))), (4, ((4, (1, 0)),)), (5, ((6, None),)), (6, ())),
-    (2, 0): ((0, ((0, None),)), (2, ((4, (0, 0)),)), (6, ((6, (0, 0)),)), (4, ())),
-    (2, 1): ((1, ((1, None), (3, None))), (3, ((5, None),)), (7, ((7, None),)), (5, ())),
+    (0, 0): ((0, ()), (2, ((2, ((1, 1),)),)), (4, ((4, ()),)), (6, ((6, ()),))),
+    (0, 1): ((1, ((1, ((2, 1),)),)), (3, ((3, ()),)), (5, ((5, ()),)), (7, ((7, ()),))),
+    (1, 0): ((0, ((0, ()),)), (7, ((7, ((0, 1),)),))),
+    (1, 1): ((1, ((3, ((0, 1),)), (2, ()))), (2, ())),
+    (2, 0): (
+        (0, ((0, ()),)),
+        (2, ((4, ((0, 0), (3, 0))),)),
+        (6, ((6, ((0, 0), (3, 1))),)),
+        (4, ()),
+    ),
+    (2, 1): ((1, ((3, ()), (1, ()))), (3, ((5, ()),)), (7, ((7, ()),)), (5, ())),
+    (3, 0): ((3, ((5, ((2, 1), (0, 1), (3, 1))), (4, ()))), (4, ())),
+    (3, 1): ((5, ((7, ((1, 0), (2, 1))), (5, ()), (6, ()))), (6, ())),
 }
+LENT = 1
+LENT_TO = 3
+WCHUNKS = 3
 HUB = (0, 1)
 ACTIONS = 3
 CHUNKS = 2
@@ -46,12 +55,11 @@
                 to.setdefault(target, set()).add((blk, core))
     for worker, units in UNITS.items():
         for _, actions in units:
-            for _, target in actions:
-                if target is not None:
+            for _, targets in actions:
+                for target in targets:
                     to.setdefault(target, set()).add(worker)
-    for router, (_, targets) in ROUTE.items():
-        for target in targets:
-            to.setdefault(target, set()).add(router)
+    for core in range(2):
+        to.setdefault((LENT_TO, core), set()).update({(LENT, core), (LENT_TO, 1 - core)})
     for blk in range(8):
         for core in range(2):
             if (blk, core) != HUB:
@@ -142,7 +150,7 @@
     count, scale_d, scale_x,
     piece_ref, hay_ref, weight_ref, map_ref, coul_ref, out_ref,
     pbuf, hbuf, wbuf, mbuf, coul, sel, fbuf, spread, stage, res, xbuf, ybuf,
-    load_sem, recv_sem, recv_hay, send_sem, send_hay, send_res, recv_res, send_x, recv_x, send_y, recv_y,
+    load_sem, recv_sem, recv_hay, recv_w, send_w, send_sem, send_hay, send_res, recv_res, send_x, recv_x, send_y, recv_y,
 ):
     grp = lax.axis_index("grp")
     me = lax.axis_index("blk")
@@ -152,7 +160,9 @@
     planes = weight_ref.shape[1]
     edge = count * NV
     hub = HUB[0] * 2 + HUB[1]
-    worker = me < STOPS + 1
+    holder = me < STOPS + 1
+    worker = holder | (me == LENT_TO)
+    stop = jnp.where(me == LENT_TO, LENT, me)
     chunk = 2 * edge // CHUNKS
 
     def each(n, body):
@@ -196,7 +206,7 @@
     for load in loads[:4]:
         load.start()
 
-    @pl.when(worker)
+    @pl.when(holder)
     def _():
         loads[4].start()
 
@@ -241,6 +251,32 @@
             ).start())
 
     each(3, own_slot)
+    half = planes // 2
+    share = half // WCHUNKS
+
+    def lent_rows(core, c):
+        return pl.ds(pl.multiple_of(core * half + c * share, share), share)
+
+    @pl.when(me == LENT)
+    def _():
+        each(WCHUNKS, lambda c: remote(
+            weight_ref.at[0, lent_rows(p, c)], wbuf.at[lent_rows(p, c)],
+            send_w, recv_w.at[p, c], LENT_TO * 2 + p,
+        ).start())
+
+    def take_lent():
+        def own_half(c):
+            ref = wbuf.at[lent_rows(p, c)]
+            pltpu.make_async_copy(ref, ref, recv_w.at[p, c]).wait()
+            remote(ref, ref, send_w, recv_w.at[p, c], LENT_TO * 2 + 1 - p).start()
+
+        def other_half(c):
+            ref = wbuf.at[lent_rows(1 - p, c)]
+            pltpu.make_async_copy(ref, ref, recv_w.at[1 - p, c]).wait()
+
+        each(WCHUNKS, own_half)
+        each(WCHUNKS, other_half)
+
 
     spread[...] = spread_matrix(edge)
     for load in loads[:4]:
@@ -281,36 +317,79 @@
         each(CHUNKS, per_chunk)
 
     def res_copy(t, b, core):
-        return remote(stage.at[t], res.at[me], send_res, recv_res, b * 2 + core)
-
-    partners = [0] * 24
-    codes = [0] * (24 * ACTIONS)
-    for (s, core), units in UNITS.items():
+        return remote(stage.at[t], res.at[stop], send_res, recv_res, b * 2 + core)
+
+    partners = [0] * 32
+    codes = [0] * (32 * ACTIONS)
+    passed = [0] * 16
+    results = [0] * 16
+    for (blk, core), units in UNITS.items():
+        d = blk * 2 + core
+        results[d] = 2 * len(units) - (blk <= STOPS and core == 0)
         for t, (i, actions) in enumerate(units):
-            at = (s * 2 + core) * 4 + t
-            partners[at] = i
-            for n, (b, target) in enumerate(actions):
-                onward = 0 if target is None else target[0] * 2 + target[1] + 1
-                codes[at * ACTIONS + n] = 1 + b + 8 * onward
-
-    def unit_of(t):
-        i = lut(dev * 4 + t, partners)
-        return i, (i + me) % blocks
-
-    def action_of(t, n):
-        code = lut((dev * 4 + t) * ACTIONS + n, codes)
-        packed = jnp.maximum(code - 1, 0)
-        onward = packed // 8
-        return code > 0, packed % 8, onward > 0, jnp.maximum(onward - 1, 0)
+            partners[d * 4 + t] = i + 1
+            for n, (b, targets) in enumerate(actions):
+                code = 0
+                for target in reversed(targets):
+                    code = code * 17 + target[0] * 2 + target[1] + 1
+                codes[(d * 4 + t) * ACTIONS + n] = 1 + b + 8 * code
+                passed[d] += len(targets)
+
+    def unit(t, i):
+        b = (i + stop) % blocks
+        mix_i = make_mix(hbuf[i, :count], spread[...], count)
+        amp_i = dot_nn(mix_i, pbuf[i, 0]).astype(jnp.bfloat16)
+        perm = dot_nn(jnp.concatenate([amp_i, pbuf[i, 1]], axis=0), sel[...])
+        cond_t = perm[2 * edge :].T.astype(jnp.bfloat16)
+        turned = jnp.concatenate([perm[edge : 2 * edge], -perm[:edge]], axis=0)
+        both = jnp.concatenate([perm[: 2 * edge], turned], axis=1).astype(jnp.bfloat16)
+        val_b = pbuf[b, 0]
+        swapped = jnp.concatenate([-val_b[edge:], val_b[:edge]], axis=0)
+        v_lanes = jnp.concatenate(
+            [
+                jnp.concatenate([val_b[:edge], swapped[:edge]], axis=0),
+                jnp.concatenate([val_b[edge:], swapped[edge:]], axis=0),
+            ],
+            axis=1,
+        )
+
+        @pl.when((me == LENT_TO) & (t == 0))
+        def _():
+            take_lent()
+
+        tile = 256
+        for r in range(planes // tile):
+            rows = slice(r * tile, (r + 1) * tile)
+            w = wbuf[rows, :].astype(jnp.float32)
+            h = (dot_nn(cond_t[rows], both) * jnp.concatenate([w, w], axis=1)).astype(jnp.bfloat16)
+            fbuf[rows, :] = dot_nt(h, v_lanes).astype(jnp.bfloat16)
+        part = fold_block(dot_nn(pbuf[b, 1], fbuf[...]), count) * scale_d
+        stage[t, :, : 2 * edge] = part
+
+        @pl.when((b == me) & (p == 0))
+        def _():
+            res[stop, :, : 2 * edge] = part
+
+
+        def send_result(core):
+            @pl.when(jnp.logical_not((b == me) & (p == core)))
+            def _():
+                res_copy(t, b, core).start()
+
+        each(2, send_result)
+
 
     fifteen = xbuf.at[pl.ds(0, 15)]
 
     @pl.when(worker)
     def _():
         sel[...] = jnp.where(
-            mbuf[pl.ds(me, 1), :] == iota((planes, planes), 0), 1.0, 0.0
+            mbuf[pl.ds(stop, 1), :] == iota((planes, planes), 0), 1.0, 0.0
         ).astype(jnp.bfloat16)
-        loads[4].wait()
+
+        @pl.when(holder)
+        def _():
+            loads[4].wait()
 
         def step(t):
             @pl.when((dev == hub) & (t == 1))
@@ -321,62 +400,32 @@
                 others(lambda d: y_copy(d).start())
 
             def act(n):
-                go, b, onward, target = action_of(t, n)
+                code = lut((dev * 4 + t) * ACTIONS + n, codes)
+                packed = jnp.maximum(code - 1, 0)
+                onward = packed // 8
 
                 def pass_on(start):
-                    @pl.when(onward)
-                    def _():
-                        start(target)
-
-                @pl.when(go)
+                    def per_target(slot):
+                        target = onward // lut(slot, [1, 17, 289]) % 17
+
+                        @pl.when(target > 0)
+                        def _():
+                            start(jnp.maximum(target - 1, 0))
+
+                    each(3, per_target)
+
+                @pl.when(code > 0)
                 def _():
-                    arrive(b, pass_on)
+                    arrive(packed % 8, pass_on)
 
             each(ACTIONS, act)
-            i, b = unit_of(t)
-            mix_i = make_mix(hbuf[i, :count], spread[...], count)
-            amp_i = dot_nn(mix_i, pbuf[i, 0]).astype(jnp.bfloat16)
-            perm = dot_nn(jnp.concatenate([amp_i, pbuf[i, 1]], axis=0), sel[...])
-            cond_t = perm[2 * edge :].T.astype(jnp.bfloat16)
-            turned = jnp.concatenate([perm[edge : 2 * edge], -perm[:edge]], axis=0)
-            both = jnp.concatenate([perm[: 2 * edge], turned], axis=1).astype(jnp.bfloat16)
-            val_b = pbuf[b, 0]
-            swapped = jnp.concatenate([-val_b[edge:], val_b[:edge]], axis=0)
-            v_lanes = jnp.concatenate(
-                [
-                    jnp.concatenate([val_b[:edge], swapped[:edge]], axis=0),
-                    jnp.concatenate([val_b[edge:], swapped[edge:]], axis=0),
-                ],
-                axis=1,
-            )
-            tile = 256
-            for r in range(planes // tile):
-                rows = slice(r * tile, (r + 1) * tile)
-                w = wbuf[rows, :].astype(jnp.float32)
-                h = (dot_nn(cond_t[rows], both) * jnp.concatenate([w, w], axis=1)).astype(jnp.bfloat16)
-                fbuf[rows, :] = dot_nt(h, v_lanes).astype(jnp.bfloat16)
-            part = fold_block(dot_nn(pbuf[b, 1], fbuf[...]), count) * scale_d
-            stage[t, :, : 2 * edge] = part
-
-            @pl.when((b == me) & (p == 0))
+            i = lut(dev * 4 + t, partners) - 1
+
+            @pl.when(i >= 0)
             def _():
-                res[me, :, : 2 * edge] = part
-
-
-            def send_result(core):
-                @pl.when(jnp.logical_not((b == me) & (p == core)))
-                def _():
-                    res_copy(t, b, core).start()
-
-            each(2, send_result)
+                unit(t, jnp.maximum(i, 0))
 
         each(4, step)
-
-    routed = 5 + 2 * p
-
-    @pl.when(me == 3)
-    def _():
-        arrive(routed, lambda start: each(2, lambda slot: start(3 + 2 * slot)))
 
     @pl.when(dev != hub)
     def _():
@@ -388,7 +437,7 @@
     f_rows = jnp.concatenate([y_re * v_re + y_im * v_im, y_im * v_re - y_re * v_im], axis=0)
     total = fold_block(dot_nt(pbuf[me, 1], f_rows.astype(jnp.bfloat16)), count)
 
-    awaited = jnp.where((p == 0) & worker, STOPS, STOPS + 1)
+    awaited = jnp.where((p == 0) & holder, STOPS, STOPS + 1)
     drained(awaited, STOPS + 1, lambda n: res.at[pl.ds(0, n)], recv_res)
     for s in range(STOPS + 1):
         total = total + res[s, :, : 2 * edge]
@@ -397,14 +446,9 @@
     own_count = lut(me, [len(OWN[m]) for m in range(8)])
     drained(own_count, 3, lambda n: pbuf.at[pl.ds(0, n), 0], send_sem.at[0])
     drained(jnp.where(p == 0, own_count, 0), 3, lambda n: hbuf.at[pl.ds(0, n), pl.ds(0, count)], send_hay.at[0])
-    passed = [0] * 16
-    for (s, core), units in UNITS.items():
-        passed[s * 2 + core] = sum(target is not None for _, actions in units for _, target in actions)
-    for (blk, core), (_, targets) in ROUTE.items():
-        passed[blk * 2 + core] = len(targets)
     passed = lut(dev, passed)
-    drained(passed, 3, lambda n: pbuf.at[pl.ds(0, n)], send_sem.at[1])
-    drained(passed, 3, lambda n: hbuf.at[pl.ds(0, n), pl.ds(0, count)], send_hay.at[1])
+    drained(passed, 4, lambda n: pbuf.at[pl.ds(0, n)], send_sem.at[1])
+    drained(passed, 4, lambda n: hbuf.at[pl.ds(0, n), pl.ds(0, count)], send_hay.at[1])
 
     @pl.when(dev != hub)
     def _():
@@ -414,10 +458,11 @@
     def _():
         pltpu.make_async_copy(fifteen, fifteen, send_y).wait()
 
-    for n in (7, 8):
-        @pl.when(worker & (8 - n == 1 - p))
-        def _():
-            pltpu.make_async_copy(stage.at[pl.ds(0, n)], stage.at[pl.ds(0, n)], send_res).wait()
+    drained(lut(dev, results), 8, lambda n: stage.at[pl.ds(0, n)], send_res)
+
+    @pl.when((me == LENT) | (me == LENT_TO))
+    def _():
+        pltpu.make_async_copy(wbuf.at[pl.ds(0, half)], wbuf.at[pl.ds(0, half)], send_w).wait()
 
 
 def scales(planes, count, total_k):
@@ -460,6 +505,8 @@
             dma((5,)),
             dma((blocks, CHUNKS)),
             dma((blocks,)),
+            dma((2, WCHUNKS)),
+            dma,
             dma((2,)),
             dma((2,)),
             dma,

time: 33.6 us -> 31.2 us (0.929)
  the two profiles are of different devices: /device:TPU:27 before, /device:TPU:19 now
where the time goes in v3:
time: 31.2 us; the launch traced here: 31 us
  Pallas kernels  28 us (90%)
  local copies, waits for them, and re-layouts  2.97 us (10%)
    pallas_call x1, Pallas kernels, per_device(): pl.pallas_call(functools.partial(kernel, count, scale_d, scale_x), out_sh...  28 us
    reshape x1, local copies, waits for them, and re-layouts, rows_of(): rows = wave.reshape(count, 2, NV, 2, planes).transpose(1, 3, 0, 2, 4)  1.7 us
    unnamed x1, local copies, waits for them, and re-layouts  1.28 us

profile of v3, /device:TPU:19, one launch (start us, length us, event | category | flops | bytes accessed | tf_op | source)
XLA Modules:
  0.0 31.0 jit_solution(2817878731419544509)
XLA Ops:
  0.0 1.7 %copy.6 = bf16[6,2,8,2,768]{4,2,0,3,1:T(8,128)(2,1)} copy(bf16[6,2,8,2,768]{4,3,2,1,0:T(2,128)(2,1)} %bitcast.6) | data formatting | bytes 589824 | tf_op jit(solution)/shard_map/reshape | solution.py:477
  1.7 28.0 %shard_map.55 = f32[6,128]{1,0:T(8,128)} custom-call(bf16[2,96,768]{2,1,0:T(8,128)(2,1)} %bitcast.5, f32[6,128]{1,0:T(8,128)} %hay_ref.1, bf16[1,768,768]{2,1,0:T(8,128)(2,1)} %weight_ref.1, s32[3,768]{1,0:T(4,128)} %map_ref.1, f32[6,128]{1,0:T(8,128)} %bitcast.7), custom_call_target="tpu_custom_call" | custom-call | tf_op jit(solution)/shard_map/pallas_call | solution.py:487
  29.7 1.3 %copy.8 = f32[6,128]{1,0:T(8,128)} copy(f32[6,128]{1,0:T(8,128)} %shard_map.55) | data formatting | bytes 6144

commit v4 on v3

--- a/solution.py
+++ b/solution.py
@@ -25,26 +25,21 @@
     7: ((3, 1),),
 }
 UNITS = {
-    (0, 0): ((0, ()), (2, ((2, ((1, 1),)),)), (4, ((4, ()),)), (6, ((6, ()),))),
-    (0, 1): ((1, ((1, ((2, 1),)),)), (3, ((3, ()),)), (5, ((5, ()),)), (7, ((7, ()),))),
-    (1, 0): ((0, ((0, ()),)), (7, ((7, ((0, 1),)),))),
-    (1, 1): ((1, ((3, ((0, 1),)), (2, ()))), (2, ())),
-    (2, 0): (
-        (0, ((0, ()),)),
-        (2, ((4, ((0, 0), (3, 0))),)),
-        (6, ((6, ((0, 0), (3, 1))),)),
-        (4, ()),
-    ),
-    (2, 1): ((1, ((3, ()), (1, ()))), (3, ((5, ()),)), (7, ((7, ()),)), (5, ())),
-    (3, 0): ((3, ((5, ((2, 1), (0, 1), (3, 1))), (4, ()))), (4, ())),
-    (3, 1): ((5, ((7, ((1, 0), (2, 1))), (5, ()), (6, ()))), (6, ())),
+    (0, 0): (((0, 2), ((2, ((1, 1),)),)), ((4, 6), ((4, ()), (6, ())))),
+    (0, 1): (((1, 3), ((1, ((2, 1),)), (3, ()))), ((5, 7), ((5, ()), (7, ())))),
+    (1, 0): (((0, 7), ((0, ()), (7, ((0, 1),)))),),
+    (1, 1): (((1, 2), ((3, ((0, 1),)), (2, ()))),),
+    (2, 0): (((6, 4), ((4, ((0, 0), (3, 0))), (6, ((0, 0), (3, 1))), (0, ()))), ((0, 2), ())),
+    (2, 1): (((7, 1), ((3, ()), (1, ()), (7, ()))), ((3, 5), ((5, ()),))),
+    (3, 0): (((3, 4), ((5, ((2, 1), (0, 1), (3, 1))), (4, ()))),),
+    (3, 1): (((5, 6), ((7, ((1, 0), (2, 1))), (5, ()), (6, ()))),),
 }
 LENT = 1
 LENT_TO = 3
 WCHUNKS = 3
 HUB = (0, 1)
 ACTIONS = 3
-CHUNKS = 2
+CHUNKS = 3
 
 
 def edges():
@@ -183,7 +178,7 @@
 
     def greet(other):
         mask = lut(other, masks)
-        power = lut(dev, [1 << d for d in range(8)])
+        power = lut(dev, [1 << d for d in range(16)])
 
         @pl.when((power > 0) & (mask // jnp.maximum(power, 1) % 2 == 1))
         def _():
@@ -250,7 +245,6 @@
                 send_sem.at[0], recv_sem.at[me, c], target,
             ).start())
 
-    each(3, own_slot)
     half = planes // 2
     share = half // WCHUNKS
 
@@ -264,19 +258,22 @@
             send_w, recv_w.at[p, c], LENT_TO * 2 + p,
         ).start())
 
-    def take_lent():
-        def own_half(c):
+    each(3, own_slot)
+
+    def take_own():
+        def per_chunk(c):
             ref = wbuf.at[lent_rows(p, c)]
             pltpu.make_async_copy(ref, ref, recv_w.at[p, c]).wait()
             remote(ref, ref, send_w, recv_w.at[p, c], LENT_TO * 2 + 1 - p).start()
 
-        def other_half(c):
+        each(WCHUNKS, per_chunk)
+
+    def take_other():
+        def per_chunk(c):
             ref = wbuf.at[lent_rows(1 - p, c)]
             pltpu.make_async_copy(ref, ref, recv_w.at[1 - p, c]).wait()
 
-        each(WCHUNKS, own_half)
-        each(WCHUNKS, other_half)
-
+        each(WCHUNKS, per_chunk)
 
     spread[...] = spread_matrix(edge)
     for load in loads[:4]:
@@ -319,31 +316,31 @@
     def res_copy(t, b, core):
         return remote(stage.at[t], res.at[stop], send_res, recv_res, b * 2 + core)
 
-    partners = [0] * 32
+    partners = [0] * 64
     codes = [0] * (32 * ACTIONS)
     passed = [0] * 16
     results = [0] * 16
-    for (blk, core), units in UNITS.items():
+    for (blk, core), steps in UNITS.items():
         d = blk * 2 + core
-        results[d] = 2 * len(units) - (blk <= STOPS and core == 0)
-        for t, (i, actions) in enumerate(units):
-            partners[d * 4 + t] = i + 1
+        results[d] = 4 * len(steps) - (blk <= STOPS and core == 0)
+        for t, (units, actions) in enumerate(steps):
+            for u, i in enumerate(units):
+                partners[d * 4 + t * 2 + u] = i + 1
             for n, (b, targets) in enumerate(actions):
                 code = 0
                 for target in reversed(targets):
                     code = code * 17 + target[0] * 2 + target[1] + 1
-                codes[(d * 4 + t) * ACTIONS + n] = 1 + b + 8 * code
+                codes[(d * 2 + t) * ACTIONS + n] = 1 + b + 8 * code
                 passed[d] += len(targets)
 
-    def unit(t, i):
-        b = (i + stop) % blocks
+    def prepare(i):
         mix_i = make_mix(hbuf[i, :count], spread[...], count)
         amp_i = dot_nn(mix_i, pbuf[i, 0]).astype(jnp.bfloat16)
         perm = dot_nn(jnp.concatenate([amp_i, pbuf[i, 1]], axis=0), sel[...])
         cond_t = perm[2 * edge :].T.astype(jnp.bfloat16)
         turned = jnp.concatenate([perm[edge : 2 * edge], -perm[:edge]], axis=0)
         both = jnp.concatenate([perm[: 2 * edge], turned], axis=1).astype(jnp.bfloat16)
-        val_b = pbuf[b, 0]
+        val_b = pbuf[(i + stop) % blocks, 0]
         swapped = jnp.concatenate([-val_b[edge:], val_b[:edge]], axis=0)
         v_lanes = jnp.concatenate(
             [
@@ -352,32 +349,38 @@
             ],
             axis=1,
         )
-
-        @pl.when((me == LENT_TO) & (t == 0))
+        return cond_t, both, v_lanes
+
+    def fold_tile(cond_t, both, v_lanes, w):
+        h = (dot_nn(cond_t, both) * jnp.concatenate([w, w], axis=1)).astype(jnp.bfloat16)
+        return dot_nt(h, v_lanes).astype(jnp.bfloat16)
+
+    def finish(t, i, f_rows):
+        b = (i + stop) % blocks
+        part = fold_block(dot_nn(pbuf[b, 1], f_rows), count) * scale_d
+        stage[t, :, : 2 * edge] = part
+
+        @pl.when((b == me) & (p == 0))
         def _():
-            take_lent()
-
+            res[stop, :, : 2 * edge] = part
+
+        def send_result(core):
+            @pl.when(jnp.logical_not((b == me) & (p == core)))
+            def _():
+                res_copy(t, b, core).start()
+
+        each(2, send_result)
+
+    def pair(t, partner):
+        ready = [prepare(partner[u]) for u in range(2)]
         tile = 256
         for r in range(planes // tile):
             rows = slice(r * tile, (r + 1) * tile)
             w = wbuf[rows, :].astype(jnp.float32)
-            h = (dot_nn(cond_t[rows], both) * jnp.concatenate([w, w], axis=1)).astype(jnp.bfloat16)
-            fbuf[rows, :] = dot_nt(h, v_lanes).astype(jnp.bfloat16)
-        part = fold_block(dot_nn(pbuf[b, 1], fbuf[...]), count) * scale_d
-        stage[t, :, : 2 * edge] = part
-
-        @pl.when((b == me) & (p == 0))
-        def _():
-            res[stop, :, : 2 * edge] = part
-
-
-        def send_result(core):
-            @pl.when(jnp.logical_not((b == me) & (p == core)))
-            def _():
-                res_copy(t, b, core).start()
-
-        each(2, send_result)
-
+            for u, (cond_t, both, v_lanes) in enumerate(ready):
+                fbuf[u, rows, :] = fold_tile(cond_t[rows], both, v_lanes, w)
+        for u in range(2):
+            finish(2 * t + u, partner[u], fbuf[u])
 
     fifteen = xbuf.at[pl.ds(0, 15)]
 
@@ -392,15 +395,19 @@
             loads[4].wait()
 
         def step(t):
-            @pl.when((dev == hub) & (t == 1))
-            def _():
-                pltpu.make_async_copy(fifteen, fifteen, recv_x).wait()
-                coul_row = jnp.concatenate([coul[n : n + 1, :] for n in range(planes // 128)], axis=1)
-                ybuf[...] = jnp.sum(xbuf[...], axis=0) * coul_row * (0.5 * scale_x)
-                others(lambda d: y_copy(d).start())
-
             def act(n):
-                code = lut((dev * 4 + t) * ACTIONS + n, codes)
+                @pl.when((dev == hub) & (t == 0) & (n == 1))
+                def _():
+                    pltpu.make_async_copy(fifteen, fifteen, recv_x).wait()
+                    coul_row = jnp.concatenate([coul[k : k + 1, :] for k in range(planes // 128)], axis=1)
+                    ybuf[...] = jnp.sum(xbuf[...], axis=0) * coul_row * (0.5 * scale_x)
+                    others(lambda d: y_copy(d).start())
+
+                @pl.when((me == LENT_TO) & (t == 0) & (n == 1))
+                def _():
+                    take_own()
+
+                code = lut((dev * 2 + t) * ACTIONS + n, codes)
                 packed = jnp.maximum(code - 1, 0)
                 onward = packed // 8
 
@@ -419,13 +426,18 @@
                     arrive(packed % 8, pass_on)
 
             each(ACTIONS, act)
-            i = lut(dev * 4 + t, partners) - 1
-
-            @pl.when(i >= 0)
+
+            partner = [lut(dev * 4 + 2 * t + u, partners) - 1 for u in range(2)]
+
+            @pl.when((me == LENT_TO) & (t == 0))
             def _():
-                unit(t, jnp.maximum(i, 0))
-
-        each(4, step)
+                take_other()
+
+            @pl.when(partner[0] >= 0)
+            def _():
+                pair(t, [jnp.maximum(i, 0) for i in partner])
+
+        each(2, step)
 
     @pl.when(dev != hub)
     def _():
@@ -496,7 +508,7 @@
             pltpu.VMEM((STOPS + 1, planes), jnp.int32),
             pltpu.VMEM((planes // 128, 128), jnp.float32),
             pltpu.VMEM((planes, planes), jnp.bfloat16),
-            pltpu.VMEM((planes, 2 * edge), jnp.bfloat16),
+            pltpu.VMEM((2, planes, 2 * edge), jnp.bfloat16),
             pltpu.VMEM((128, 256), jnp.bfloat16),
             pltpu.VMEM((8, 2 * NV, 128), jnp.float32),
             pltpu.VMEM((STOPS + 1, 2 * NV, 128), jnp.float32),

time: 31.2 us -> 28.8 us (0.923)
  the two profiles are of different devices: /device:TPU:19 before, /device:TPU:0 now
where the time goes in v4:
time: 28.8 us; the launch traced here: 28.6 us
  Pallas kernels  25.6 us (89%)
  local copies, waits for them, and re-layouts  2.97 us (10%)
    pallas_call x1, Pallas kernels, per_device(): pl.pallas_call(functools.partial(kernel, count, scale_d, scale_x), out_sh...  25.6 us
    reshape x1, local copies, waits for them, and re-layouts, rows_of(): rows = wave.reshape(count, 2, NV, 2, planes).transpose(1, 3, 0, 2, 4)  1.7 us
    unnamed x1, local copies, waits for them, and re-layouts  1.28 us

profile of v4, /device:TPU:0, one launch (start us, length us, event | category | flops | bytes accessed | tf_op | source)
XLA Modules:
  0.0 28.6 jit_solution(12607315153078263224)
XLA Ops:
  0.0 1.7 %copy.6 = bf16[6,2,8,2,768]{4,2,0,3,1:T(8,128)(2,1)} copy(bf16[6,2,8,2,768]{4,3,2,1,0:T(2,128)(2,1)} %bitcast.6) | data formatting | bytes 589824 | tf_op jit(solution)/shard_map/reshape | solution.py:489
  1.7 25.6 %shard_map.55 = f32[6,128]{1,0:T(8,128)} custom-call(bf16[2,96,768]{2,1,0:T(8,128)(2,1)} %bitcast.5, f32[6,128]{1,0:T(8,128)} %hay_ref.1, bf16[1,768,768]{2,1,0:T(8,128)(2,1)} %weight_ref.1, s32[3,768]{1,0:T(4,128)} %map_ref.1, f32[6,128]{1,0:T(8,128)} %bitcast.7), custom_call_target="tpu_custom_call" | custom-call | tf_op jit(solution)/shard_map/pallas_call | solution.py:499
  27.3 1.3 %copy.8 = f32[6,128]{1,0:T(8,128)} copy(f32[6,128]{1,0:T(8,128)} %shard_map.55) | data formatting | bytes 6144

commit v5 on v4

--- a/solution.py
+++ b/solution.py
@@ -29,7 +29,7 @@
     (0, 1): (((1, 3), ((1, ((2, 1),)), (3, ()))), ((5, 7), ((5, ()), (7, ())))),
     (1, 0): (((0, 7), ((0, ()), (7, ((0, 1),)))),),
     (1, 1): (((1, 2), ((3, ((0, 1),)), (2, ()))),),
-    (2, 0): (((6, 4), ((4, ((0, 0), (3, 0))), (6, ((0, 0), (3, 1))), (0, ()))), ((0, 2), ())),
+    (2, 0): (((6, 4), ((6, ((0, 0), (3, 1))), (4, ((0, 0), (3, 0))), (0, ()))), ((0, 2), ())),
     (2, 1): (((7, 1), ((3, ()), (1, ()), (7, ()))), ((3, 5), ((5, ()),))),
     (3, 0): (((3, 4), ((5, ((2, 1), (0, 1), (3, 1))), (4, ()))),),
     (3, 1): (((5, 6), ((7, ((1, 0), (2, 1))), (5, ()), (6, ()))),),
@@ -176,15 +176,16 @@
             expect[sender[0] * 2 + sender[1]] += 1
             masks[sender[0] * 2 + sender[1]] |= 1 << (blk * 2 + core)
 
+    power = lut(dev, [1 << d for d in range(8)])
+
     def greet(other):
-        mask = lut(other, masks)
-        power = lut(dev, [1 << d for d in range(16)])
-
-        @pl.when((power > 0) & (mask // jnp.maximum(power, 1) % 2 == 1))
+        @pl.when(lut(other, masks) // jnp.maximum(power, 1) % 2 == 1)
         def _():
             pl.semaphore_signal(barrier, inc=1, device_id=(grp, other // 2, other % 2), device_id_type=MESH)
 
-    each(16, greet)
+    @pl.when(worker)
+    def _():
+        each(16, greet)
 
     loads = [
         pltpu.make_async_copy(src, dst, load_sem.at[n])

time: 28.8 us -> 28.1 us (0.976)
  the two profiles are of different devices: /device:TPU:0 before, /device:TPU:27 now
where the time goes in v5:
time: 28.1 us; the launch traced here: 27.6 us
  Pallas kernels  24.7 us (88%)
  local copies, waits for them, and re-layouts  2.97 us (11%)
    pallas_call x1, Pallas kernels, per_device(): pl.pallas_call(functools.partial(kernel, count, scale_d, scale_x), out_sh...  24.7 us
    reshape x1, local copies, waits for them, and re-layouts, rows_of(): rows = wave.reshape(count, 2, NV, 2, planes).transpose(1, 3, 0, 2, 4)  1.7 us
    unnamed x1, local copies, waits for them, and re-layouts  1.28 us

profile of v5, /device:TPU:27, one launch (start us, length us, event | category | flops | bytes accessed | tf_op | source)
XLA Modules:
  0.0 27.6 jit_solution(10185889916105598169)
XLA Ops:
  0.0 1.7 %copy.6 = bf16[6,2,8,2,768]{4,2,0,3,1:T(8,128)(2,1)} copy(bf16[6,2,8,2,768]{4,3,2,1,0:T(2,128)(2,1)} %bitcast.6) | data formatting | bytes 589824 | tf_op jit(solution)/shard_map/reshape | solution.py:490
  1.7 24.7 %shard_map.55 = f32[6,128]{1,0:T(8,128)} custom-call(bf16[2,96,768]{2,1,0:T(8,128)(2,1)} %bitcast.5, f32[6,128]{1,0:T(8,128)} %hay_ref.1, bf16[1,768,768]{2,1,0:T(8,128)(2,1)} %weight_ref.1, s32[3,768]{1,0:T(4,128)} %map_ref.1, f32[6,128]{1,0:T(8,128)} %bitcast.7), custom_call_target="tpu_custom_call" | custom-call | tf_op jit(solution)/shard_map/pallas_call | solution.py:500
  26.4 1.3 %copy.8 = f32[6,128]{1,0:T(8,128)} copy(f32[6,128]{1,0:T(8,128)} %shard_map.55) | data formatting | bytes 6144

commit v6 on v5

--- a/solution.py
+++ b/solution.py
@@ -25,8 +25,8 @@
     7: ((3, 1),),
 }
 UNITS = {
-    (0, 0): (((0, 2), ((2, ((1, 1),)),)), ((4, 6), ((4, ()), (6, ())))),
-    (0, 1): (((1, 3), ((1, ((2, 1),)), (3, ()))), ((5, 7), ((5, ()), (7, ())))),
+    (0, 0): (((0, 2), ((2, ((1, 1),)),)), ((6,), ((6, ()),)), ((4,), ((4, ()),))),
+    (0, 1): (((1, 3), ((1, ((2, 1),)), (3, ()))), ((5,), ((5, ()),)), ((7,), ((7, ()),))),
     (1, 0): (((0, 7), ((0, ()), (7, ((0, 1),)))),),
     (1, 1): (((1, 2), ((3, ((0, 1),)), (2, ()))),),
     (2, 0): (((6, 4), ((6, ((0, 0), (3, 1))), (4, ((0, 0), (3, 0))), (0, ()))), ((0, 2), ())),
@@ -37,7 +37,7 @@
 LENT = 1
 LENT_TO = 3
 WCHUNKS = 3
-HUB = (0, 1)
+HUB = (1, 0)
 ACTIONS = 3
 CHUNKS = 3
 
@@ -317,21 +317,21 @@
     def res_copy(t, b, core):
         return remote(stage.at[t], res.at[stop], send_res, recv_res, b * 2 + core)
 
-    partners = [0] * 64
-    codes = [0] * (32 * ACTIONS)
+    partners = [0] * 96
+    codes = [0] * (48 * ACTIONS)
     passed = [0] * 16
     results = [0] * 16
     for (blk, core), steps in UNITS.items():
         d = blk * 2 + core
-        results[d] = 4 * len(steps) - (blk <= STOPS and core == 0)
+        results[d] = 2 * sum(len(units) for units, _ in steps) - (blk <= STOPS and core == 0)
         for t, (units, actions) in enumerate(steps):
             for u, i in enumerate(units):
-                partners[d * 4 + t * 2 + u] = i + 1
+                partners[d * 6 + t * 2 + u] = i + 1
             for n, (b, targets) in enumerate(actions):
                 code = 0
                 for target in reversed(targets):
                     code = code * 17 + target[0] * 2 + target[1] + 1
-                codes[(d * 2 + t) * ACTIONS + n] = 1 + b + 8 * code
+                codes[(d * 3 + t) * ACTIONS + n] = 1 + b + 8 * code
                 passed[d] += len(targets)
 
     def prepare(i):
@@ -372,16 +372,16 @@
 
         each(2, send_result)
 
-    def pair(t, partner):
-        ready = [prepare(partner[u]) for u in range(2)]
+    def together(t, partner):
+        ready = [prepare(i) for i in partner]
         tile = 256
         for r in range(planes // tile):
             rows = slice(r * tile, (r + 1) * tile)
             w = wbuf[rows, :].astype(jnp.float32)
             for u, (cond_t, both, v_lanes) in enumerate(ready):
                 fbuf[u, rows, :] = fold_tile(cond_t[rows], both, v_lanes, w)
-        for u in range(2):
-            finish(2 * t + u, partner[u], fbuf[u])
+        for u, i in enumerate(partner):
+            finish(2 * t + u, i, fbuf[u])
 
     fifteen = xbuf.at[pl.ds(0, 15)]
 
@@ -408,7 +408,7 @@
                 def _():
                     take_own()
 
-                code = lut((dev * 2 + t) * ACTIONS + n, codes)
+                code = lut((dev * 3 + t) * ACTIONS + n, codes)
                 packed = jnp.maximum(code - 1, 0)
                 onward = packed // 8
 
@@ -428,17 +428,18 @@
 
             each(ACTIONS, act)
 
-            partner = [lut(dev * 4 + 2 * t + u, partners) - 1 for u in range(2)]
+            partner = [lut(dev * 6 + 2 * t + u, partners) - 1 for u in range(2)]
 
             @pl.when((me == LENT_TO) & (t == 0))
             def _():
                 take_other()
 
-            @pl.when(partner[0] >= 0)
-            def _():
-                pair(t, [jnp.maximum(i, 0) for i in partner])
-
-        each(2, step)
+            for n in (1, 2):
+                @pl.when((partner[0] >= 0) & ((partner[1] >= 0) == (n == 2)))
+                def _():
+                    together(t, [jnp.maximum(i, 0) for i in partner[:n]])
+
+        each(3, step)
 
     @pl.when(dev != hub)
     def _():

time: 28.1 us -> 27.2 us (0.968)
  the two profiles are of different devices: /device:TPU:27 before, /device:TPU:25 now
where the time goes in v6:
time: 27.2 us; the launch traced here: 27 us
  Pallas kernels  24.1 us (89%)
  local copies, waits for them, and re-layouts  2.97 us (11%)
    pallas_call x1, Pallas kernels, per_device(): pl.pallas_call(functools.partial(kernel, count, scale_d, scale_x), out_sh...  24.1 us
    reshape x1, local copies, waits for them, and re-layouts, rows_of(): rows = wave.reshape(count, 2, NV, 2, planes).transpose(1, 3, 0, 2, 4)  1.7 us
    unnamed x1, local copies, waits for them, and re-layouts  1.28 us

profile of v6, /device:TPU:25, one launch (start us, length us, event | category | flops | bytes accessed | tf_op | source)
XLA Modules:
  0.0 27.0 jit_solution(16570598108278321725)
XLA Ops:
  0.0 1.7 %copy.6 = bf16[6,2,8,2,768]{4,2,0,3,1:T(8,128)(2,1)} copy(bf16[6,2,8,2,768]{4,3,2,1,0:T(2,128)(2,1)} %bitcast.6) | data formatting | bytes 589824 | tf_op jit(solution)/shard_map/reshape | solution.py:491
  1.7 24.1 %shard_map.55 = f32[6,128]{1,0:T(8,128)} custom-call(bf16[2,96,768]{2,1,0:T(8,128)(2,1)} %bitcast.5, f32[6,128]{1,0:T(8,128)} %hay_ref.1, bf16[1,768,768]{2,1,0:T(8,128)(2,1)} %weight_ref.1, s32[3,768]{1,0:T(4,128)} %map_ref.1, f32[6,128]{1,0:T(8,128)} %bitcast.7), custom_call_target="tpu_custom_call" | custom-call | tf_op jit(solution)/shard_map/pallas_call | solution.py:501
  25.8 1.3 %copy.8 = f32[6,128]{1,0:T(8,128)} copy(f32[6,128]{1,0:T(8,128)} %shard_map.55) | data formatting | bytes 6144
